TPU v7x, 32 devices: a whole 2x2x4 slice. The times are simulated.
32 devices in a mesh: wide: 8 (over z, x), narrow: 4 (over y, core).
Axes of the slice: x: 2, y: 2, z: 4, core: 2. Of those that a mesh axis runs over, the one named last changes fastest.
Arguments:
- projected: bfloat16 [3, 32768, 768], P(None, ('wide', 'narrow')), may hold values from -2.390625 to 2.390625
- layer_input: bfloat16 [32768, 768], P(('wide', 'narrow')), may hold values from -6 to 6
- segment_ids: int32 [32768], P(('wide', 'narrow')), may hold values from 0 to 2, as said below
- pad_mask: int32 [32768], P(('wide', 'narrow')), may hold values from 0 to 1, as said below
- roles: int32 [256, 3], P(('wide', 'narrow')), may hold values from 0 to 2, each once within a row
- labelled: int32 [256], P(('wide', 'narrow')), may hold values from 0 to 1, as said below
- out_weight: float32 [768, 768], replicated, may hold values from -1.75 to 1.75
- out_momentum: float32 [768, 768], replicated, may hold values from -7.6293945e-05 to 7.6293945e-05
- errors: float32 [32, 768, 768], P(('wide', 'narrow')), may hold values from -0.009765625 to 0.009765625
- factors: float32 [8, 768], replicated, may hold values from -6 to 6
- norm_gain: float32 [768], replicated, may hold values from 0.5 to 1.5
- position_bias: float32 [32, 12], replicated, may hold values from -3 to 3
- log_scale: float32 [1], replicated, may hold values from 3 to 3.6
- gain_momentum: float32 [768], replicated, may hold values from -0.0007324219 to 0.0007324219
- bias_momentum: float32 [32, 12], replicated, may hold values from -0.0014648438 to 0.0014648438
- scale_momentum: float32 [1], replicated, may hold values from -0.02 to 0.02
Outputs:
- updated_weight: float32 [768, 768], replicated
- weight_momentum: float32 [768, 768], replicated
- updated_errors: float32 [32, 768, 768], P(('wide', 'narrow'))
- updated_factors: float32 [8, 768], replicated
- updated_vectors: float32 [1153], replicated
- vector_momentum: float32 [1153], replicated
- loss_sum: float32 [1], replicated
- live_total: float32 [1], replicated
- grad_norm: float32 [1], replicated
Inputs may be any that keep to these rules, and one draw needn't show every extreme that they name: `segment_ids`: each row holds three sentences numbered 0, 1, 2 in order, each of 8 to 40 tokens, then padding that carries number 2. `pad_mask`: 1 up to the end of the row's third sentence, 0 after it. The last triple is always labelled. `roles`: each row is a permutation of 0, 1, 2.
All inputs are finite; a program needn't handle non-finite values.
Results may differ from a plain program's by a relative error of at most 0.0011.
Values may be sent and summed in bfloat16 or wider, within the bound.
A program may use at most 128 MiB of HBM per device.

v0:
```python
import jax
import jax.numpy as jnp
import numpy as np
from jax import lax
from jax.sharding import PartitionSpec as P

D = 768
HEADS = 12
HEAD_DIM = 64
BUCKETS = 32
LEN = 128
ROWS_DEV = 8


EPSILON = 1e-06
MOMENTUM_DECAY = 0.9
CLIP_NORM = 0.01
RATE_MATRIX = 50000.0
RATE_GAIN = 4000.0
RATE_BIAS = 2000.0
RATE_SCALE = 10.0
HIGHEST_PREC = lax.Precision.HIGHEST


def bucket_onehot(length, buckets):
    relative = np.arange(length)[None, :] - np.arange(length)[:, None]
    half_count = buckets // 2
    exact_count = half_count // 2
    base_part = (relative > 0).astype(np.int64) * half_count
    distance = np.abs(relative)
    larger = exact_count + (
        np.log(np.maximum(distance, 1) / exact_count)
        / np.log(128.0 / exact_count)
        * (half_count - exact_count)
    ).astype(np.int64)
    larger = np.minimum(larger, half_count - 1)
    table = base_part + np.where(distance < exact_count, distance, larger)
    return np.eye(buckets, dtype=np.float32)[table.reshape(-1)]


def orthonormal_rows(matrix):
    result_rows = []
    for index in range(matrix.shape[0]):
        vector = matrix[index]
        for earlier in result_rows:
            vector = vector - jnp.sum(vector * earlier) * earlier
        vector = vector * lax.rsqrt(jnp.sum(vector * vector) + EPSILON)
        result_rows.append(vector)
    return jnp.stack(result_rows)


def contract_first(left, right):
    return lax.dot_general(
        left, right, (((0,), (0,)), ((), ())), preferred_element_type=jnp.float32
    )


def contract_last(left, right):
    return lax.dot_general(
        left, right, (((1,), (1,)), ((), ())), preferred_element_type=jnp.float32
    )


def attention_scores(query, keys, bias_full, allowed):
    scores = (
        jnp.einsum("rihd,rjhd->rhij", query, keys, preferred_element_type=jnp.float32)
        + bias_full[None]
    )
    return jnp.where(allowed[:, None], scores, -1000000000.0)


def local(
    projected,
    layer_input,
    segment_ids,
    pad_mask,
    roles,
    labelled,
    out_weight,
    out_momentum,
    errors,
    factors,
    norm_gain,
    position_bias,
    log_scale,
    gain_momentum,
    bias_momentum,
    scale_momentum,
):
    device_count = lax.axis_size(("wide", "narrow"))
    my_index = lax.axis_index(("wide", "narrow"))
    live_rows = labelled.astype(jnp.float32)
    table = jnp.asarray(bucket_onehot(LEN, BUCKETS))
    bias_full = (
        jnp.dot(table, position_bias, precision=HIGHEST_PREC)
        .reshape(LEN, LEN, HEADS)
        .transpose(2, 0, 1)
    )
    query = projected[0].reshape(ROWS_DEV, LEN, HEADS, HEAD_DIM)
    keys = projected[1].reshape(ROWS_DEV, LEN, HEADS, HEAD_DIM)
    values = projected[2].reshape(ROWS_DEV, LEN, HEADS, HEAD_DIM)
    segments = segment_ids.reshape(ROWS_DEV, LEN)
    present = pad_mask.reshape(ROWS_DEV, LEN) == 1
    allowed = (segments[:, :, None] == segments[:, None, :]) & present[:, None, :]
    scores = attention_scores(query, keys, bias_full, allowed)
    row_top = jnp.max(scores, axis=-1, keepdims=True)
    expon = jnp.exp(scores - row_top)
    row_total = jnp.sum(expon, axis=-1, keepdims=True)
    attn_probs = expon / row_total
    log_norm = row_top + jnp.log(row_total)
    mixed = jnp.einsum(
        "rhij,rjhd->rihd",
        attn_probs.astype(jnp.bfloat16),
        values,
        preferred_element_type=jnp.float32,
    )
    mixed = mixed.reshape(ROWS_DEV * LEN, D).astype(jnp.bfloat16)
    weight_low = out_weight.astype(jnp.bfloat16)
    hidden = layer_input.astype(jnp.float32) + jnp.dot(
        mixed, weight_low, preferred_element_type=jnp.float32
    )
    rms_inv = lax.rsqrt(jnp.mean(hidden * hidden, axis=-1, keepdims=True) + EPSILON)
    zed_rows = hidden * rms_inv
    normed = (zed_rows * norm_gain).reshape(ROWS_DEV, LEN, D)
    member = ((segments[:, None, :] == jnp.arange(3)[None, :, None]) & present[:, None, :]).astype(
        jnp.float32
    )
    counts = jnp.sum(member, axis=-1, keepdims=True)
    means = jnp.einsum("rst,rtd->rsd", member, normed, precision=HIGHEST_PREC) / counts
    inverse = lax.rsqrt(jnp.sum(means * means, axis=-1, keepdims=True) + EPSILON)
    unit_vec = means * inverse
    role_pick = (roles[:, :, None] == jnp.arange(3)[None, None, :]).astype(jnp.float32)
    chosen = jnp.einsum("rks,rsd->krd", role_pick, unit_vec, precision=HIGHEST_PREC)
    anchors = chosen[0].astype(jnp.bfloat16)
    own_cands = jnp.concatenate([chosen[1], chosen[2]], axis=0).astype(jnp.bfloat16)
    temper = jnp.exp(log_scale[0])
    live_total = lax.psum(jnp.sum(live_rows), ("wide", "narrow"))
    every_cand = lax.all_gather(own_cands, ("wide", "narrow"), axis=0, tiled=True)
    raw_scores = contract_last(anchors, every_cand)
    logits = temper * raw_scores
    logit_top = jnp.max(logits, axis=1, keepdims=True)
    log_total = logit_top[:, 0] + jnp.log(jnp.sum(jnp.exp(logits - logit_top), axis=1))
    positive_col = my_index * 2 * ROWS_DEV + jnp.arange(ROWS_DEV)
    target = (jnp.arange(logits.shape[1])[None, :] == positive_col[:, None]).astype(jnp.float32)
    own_logit = jnp.sum(logits * target, axis=1)
    loss_local = jnp.sum(live_rows * (log_total - own_logit))
    loss_weight = live_rows / live_total
    logit_grad = (jnp.exp(logits - log_total[:, None]) - target) * loss_weight[:, None]
    scale_grad = jnp.sum(logit_grad * logits)
    grad_low = (temper * logit_grad).astype(jnp.bfloat16)
    anchor_grad = jnp.dot(grad_low, every_cand, preferred_element_type=jnp.float32)
    cand_grad = lax.psum_scatter(
        contract_first(grad_low, anchors), ("wide", "narrow"), scatter_dimension=0, tiled=True
    )
    chosen_grad = jnp.stack([anchor_grad, cand_grad[:ROWS_DEV], cand_grad[ROWS_DEV:]])
    unit_grad = jnp.einsum("rks,krd->rsd", role_pick, chosen_grad, precision=HIGHEST_PREC)
    mean_grad = inverse * (
        unit_grad - unit_vec * jnp.sum(unit_vec * unit_grad, axis=-1, keepdims=True)
    )
    token_grad = jnp.einsum(
        "rst,rsd->rtd", member, mean_grad / counts, precision=HIGHEST_PREC
    ).reshape(ROWS_DEV * LEN, D)
    gain_grad = jnp.sum(token_grad * zed_rows, axis=0)
    zed_grad = token_grad * norm_gain
    hidden_grad = rms_inv * (
        zed_grad - zed_rows * jnp.mean(zed_grad * zed_rows, axis=-1, keepdims=True)
    )
    branch_grad = hidden_grad.astype(jnp.bfloat16)
    local_grad = contract_first(mixed, branch_grad)
    mixed_grad = (
        contract_last(branch_grad, weight_low)
        .astype(jnp.bfloat16)
        .reshape(ROWS_DEV, LEN, HEADS, HEAD_DIM)
    )
    again_probs = jnp.exp(attention_scores(query, keys, bias_full, allowed) - log_norm)
    prob_grad = jnp.einsum(
        "rihd,rjhd->rhij", mixed_grad, values, preferred_element_type=jnp.float32
    )
    score_grad = again_probs * (
        prob_grad - jnp.sum(again_probs * prob_grad, axis=-1, keepdims=True)
    )
    bias_total = jnp.sum(score_grad, axis=0).transpose(1, 2, 0).reshape(LEN * LEN, HEADS)
    bias_grad = lax.dot_general(table, bias_total, (((0,), (0,)), ((), ())), precision=HIGHEST_PREC)
    matrices = local_grad + errors[0]
    row_part = lax.dot_general(factors, matrices, (((1,), (1,)), ((), ())), precision=HIGHEST_PREC)
    vector_grad = jnp.concatenate([gain_grad, bias_grad.reshape(-1), scale_grad[None]])
    factor_sum, vector_sum, loss_sum = lax.psum(
        (row_part, vector_grad, loss_local), ("wide", "narrow")
    )
    ortho = orthonormal_rows(factor_sum)
    factors_new = lax.psum(jnp.dot(ortho, matrices, precision=HIGHEST_PREC), ("wide", "narrow"))
    approx = lax.dot_general(ortho, factors_new, (((0,), (0,)), ((), ())), precision=HIGHEST_PREC)
    grad_norm = jnp.sqrt(jnp.sum(approx * approx) + jnp.sum(vector_sum * vector_sum))
    clip = CLIP_NORM / jnp.maximum(grad_norm, CLIP_NORM)
    weight_mom = MOMENTUM_DECAY * out_momentum + clip * approx
    weight_new = out_weight - RATE_MATRIX * weight_mom
    errors_new = (matrices - approx / device_count)[None]
    vector_old = jnp.concatenate([norm_gain, position_bias.reshape(-1), log_scale])
    vector_mom_old = jnp.concatenate([gain_momentum, bias_momentum.reshape(-1), scale_momentum])
    vector_mom = MOMENTUM_DECAY * vector_mom_old + clip * vector_sum
    rates = jnp.concatenate(
        [
            jnp.full((D,), RATE_GAIN, jnp.float32),
            jnp.full((BUCKETS * HEADS,), RATE_BIAS, jnp.float32),
            jnp.full((1,), RATE_SCALE, jnp.float32),
        ]
    )
    vector_new = vector_old - rates * vector_mom
    return (
        weight_new,
        weight_mom,
        errors_new,
        factors_new,
        vector_new,
        vector_mom,
        loss_sum[None],
        jnp.reshape(live_total, (1,)),
        grad_norm[None],
    )


def solution(mesh):
    in_specs = (
        P(None, ("wide", "narrow"), None),
        P(("wide", "narrow"), None),
        P(("wide", "narrow")),
        P(("wide", "narrow")),
        P(("wide", "narrow"), None),
        P(("wide", "narrow")),
        P(),
        P(),
        P(("wide", "narrow"), None, None),
        P(),
        P(),
        P(),
        P(),
        P(),
        P(),
        P(),
    )
    out_specs = (P(), P(), P(("wide", "narrow"), None, None), P(), P(), P(), P(), P(), P())
    return jax.shard_map(local, mesh=mesh, in_specs=in_specs, out_specs=out_specs, check_vma=False)
```

profile of v0, /device:TPU:0, one launch (start us, length us, event | category | flops | bytes accessed | tf_op | source)
XLA Modules:
  0.0 432.4 jit_solution(17324853347763365219)
XLA Ops:
  9.8 2.8 fusion.62
  14.0 3.8 fusion.58
  17.8 2.1 copy.107
  20.0 1.8 copy.133
  21.8 1.6 copy.106
  23.4 1.8 copy.132
  25.3 2.6 copy.111
  27.9 1.9 copy.131
  29.8 1.8 fusion.60
  31.7 1.7 fusion.3
  34.3 1.3 fusion.17
  35.6 1.2 copy.114
  37.3 1.7 multiply_reduce_fusion.3
  39.7 1.2 multiply_reduce_fusion.5
  41.5 48.2 %all_gather.3 = bf16[512,768]{1,0:T(8,128)(2,1)} all-gather(bf16[16,768]{1,0:T(8,128)(2,1)S(1)} %pad_maximum_fusion.1), channel_id=1, replica_groups=mesh['wide'=8,'narrow'=4] {'wide','narrow'}, dimensions={0}, use_global_device_ids=true | all-gather | bytes 811008 | tf_op jit(solution)/shard_map/all_gather | solution.py:138
  91.0 37.3 %psum.35 = f32[]{:T(128)} all-reduce(f32[]{:T(128)} %convert_reduce_fusion.1), channel_id=1, replica_groups=mesh['wide'=8,'narrow'=4] {'wide','narrow'}, use_global_device_ids=true, to_apply=%region_8.9 | all-reduce | flops 1 | bytes 8 | tf_op jit(solution)/shard_map/psum | solution.py:137
  128.9 1.6 fusion.61
  130.7 1.6 fusion.45
  134.8 1.4 convolution_bitcast_fusion
  136.2 94.0 %reduce-scatter.2.cloned.1.call-done = f32[16,768]{1,0:T(8,128)} async-done(((f32[512,768]{1,0:T(8,128)}), f32[16,768]{1,0:T(8,128)}) %reduce-scatter.2.cloned.1.call-update) | async-done | bytes 49168 | tf_op jit(solution)/shard_map/reduce_scatter | solution.py:152
  231.4 1.5 fusion.53
  235.6 2.6 convolution_convert_fusion
  238.1 1.4 bitcast_add_fusion
  239.5 2.0 convolution_bitcast_fusion.1
  241.6 40.3 %psum.36 = f32[8,768]{1,0:T(8,128)S(1)} all-reduce(f32[8,768]{1,0:T(8,128)S(1)} %convolution_bitcast_fusion.1), channel_id=1, replica_groups=mesh['wide'=8,'narrow'=4] {'wide','narrow'}, use_global_device_ids=true, to_apply=%region_12.13 | all-reduce | flops 6144 | bytes 49152 | tf_op jit(solution)/shard_map/psum | solution.py:187
  283.8 1.3 multiply_reduce_fusion.16
  285.8 5.1 %multiply_reduce_fusion.15 = (f32[]{:T(128)}, f32[]{:T(128)}, f32[]{:T(128)}, f32[]{:T(128)}, f32[]{:T(128)}, /*index=5*/f32[]{:T(128)}, f32[768]{0:T(1024)S(1)}) fusion(f32[768]{0:T(1024)S(1)} %get-tuple-element.11, f32[768]{0:T(1024)S(1)} %get-tuple-element.82, f32[]{:T(128)} %get-tuple-element.41, f32[768]{0:T(1024)S(1)} %get-tuple-element.12, ...), kind=kLoop, calls=%fused_computation.102 | loop fusion | flops 20730 | bytes 27704 | tf_op jit(solution)/shard_map/reduce_sum | solution.py:46
  291.0 1.8 multiply_reduce_fusion.39
  293.5 2.0 multiply_reduce_fusion.36
  295.4 6.4 %multiply_reduce_fusion.14 = (f32[]{:T(128)}, f32[]{:T(128)}, f32[]{:T(128)}, f32[]{:T(128)}, f32[]{:T(128)}, /*index=5*/f32[768]{0:T(1024)S(1)}, f32[768]{0:T(1024)S(1)}, f32[768]{0:T(1024)S(1)}, f32[768]{0:T(1024)S(1)}) fusion(f32[768]{0:T(1024)S(1)} %get-tuple-element.80, f32[]{:T(128)S(6)} %rsqrt.44, f32[768]{0:T(1024)S(1)} %get-tuple-element.78, ...), kind=kLoop, calls=%fused_computation.100 | loop fusion | flops 22267 | bytes 36924 | tf_op jit(solution)/shard_map/reduce_sum | solution.py:46
  302.5 3.7 multiply_reduce_fusion.13
  306.2 2.4 multiply_reduce_fusion.30
  309.3 5.1 %multiply_reduce_fusion.12 = (f32[]{:T(128)}, f32[]{:T(128)}, f32[]{:T(128)}, f32[768]{0:T(1024)S(1)}, f32[768]{0:T(1024)S(1)}, /*index=5*/f32[768]{0:T(1024)S(1)}) fusion(f32[768]{0:T(1024)S(1)} %get-tuple-element.72, f32[]{:T(128)S(6)} %rsqrt.46, f32[]{:T(128)S(6)} %rsqrt.45, f32[768]{0:T(1024)S(1)} %get-tuple-element.78, f32[]{:T(128)} %get-tuple-element.77, ...), kind=kLoop, calls=%fused_computation.96 | loop fusion | flops 17661 | bytes 27700 | tf_op jit(solution)/shard_map/reduce_sum | solution.py:46
  316.3 1.9 multiply_reduce_fusion.11
  318.2 1.9 multiply_reduce_fusion.17
  320.7 1.9 multiply_reduce_fusion.10
  322.6 1.2 multiply_reduce_fusion.9
  324.5 17.6 %subtract_multiply_fusion.1 = (f32[1,768]{1,0:T(1,128)S(1)}, f32[1,768]{1,0:T(1,128)S(1)}, f32[1,768]{1,0:T(1,128)S(1)}, f32[1,768]{1,0:T(1,128)S(1)}, f32[1,768...) fusion(f32[1,768]{1,0:T(1,128)S(1)} %get-tuple-element.83, f32[8,768]{1,0:T(8,128)S(1)} %psum.36, ...), kind=kLoop, calls=%fused_computation.156 | loop fusion | flops 48384 | bytes 46220 | tf_op jit(solution)/shard_map/mul | solution.py:47
  342.1 1.2 fusion.63
  343.3 2.6 copy.118
  345.9 3.0 copy.136
  348.9 8.4 %fusion = f32[8,12,128,128]{2,3,1,0:T(8,128)} fusion(f32[8,12,128,128]{2,3,1,0:T(8,128)} %copy-done.1, f32[8,12,128]{2,1,0:T(8,128)S(1)} %log_add_fusion, bf16[8,128,12,64]{1,0,3,2:T(8,128)(2,1)} %bitcast.113, bf16[8,128,12,64]{1,0,3,2:T(8,128)(2,1)} %bitcast.111), kind=kOutput, calls=%fused_computation | convolution fusion | flops 204484736 | bytes 15777792 | tf_op jit(solution)/shard_map/sub | solution.py:180
  357.4 7.7 %multiply_reduce_fusion = f32[12,128,128]{1,2,0:T(8,128)S(1)} fusion(f32[8,12,128,128]{2,3,1,0:T(8,128)} %fusion, f32[8,12,128,128]{2,3,1,0:T(8,128)} %copy-done.1, f32[8,12,128]{2,1,0:T(8,128)S(1)} %log_add_fusion, bf16[8,128,12,64]{1,0,3,2:T(8,128)(2,1)} %bitcast.112, bf16[8,128,12,64]{1,0,3,2:T(8,128)(2,1)} %bitcast.114), kind=kOutput, calls=%fused_computation.2 | convolution fusion | flops 207421440 | bytes 16564224 | tf_op jit(solution)/shard_map/rihd,rjhd->rhij/dot_general | solution.py:176
  366.2 1.4 pad.14
  368.2 1.8 fusion.64
  370.7 40.2 %all-reduce = (f32[8,768]{1,0:T(8,128)S(1)}, f32[1153]{0:T(1024)S(1)}, f32[1]{0:T(128)}) all-reduce(f32[8,768]{1,0:T(8,128)S(1)} %fusion.63, f32[1153]{0:T(1024)S(1)} %pad_maximum_fusion.2, f32[1]{0:T(128)} %bitcast.16), channel_id=1, replica_groups=mesh['wide'=8,'narrow'=4] {'wide','narrow'}, use_global_device_ids=true, to_apply=%region_49.50 | all-reduce | flops 7298 | bytes 58384 | tf_op jit(solution)/shard_map/psum | solution.py:191
  410.9 4.1 multiply_reduce_fusion.4
  417.0 6.5 %multiply_subtract_fusion = (f32[768,768]{1,0:T(8,128)}, f32[768,768]{1,0:T(8,128)}, f32[1,768,768]{2,1,0:T(8,128)}) fusion(f32[768,768]{1,0:T(8,128)} %param.23, f32[768,768]{1,0:T(8,128)} %get-tuple-element.102, f32[]{:T(128)S(6)} %div.52, f32[768,768]{1,0:T(8,128)} %param.24, f32[768,768]{1,0:T(8,128)S(1)} %bitcast_add_fusion), kind=kLoop, calls=%fused_computation.22 | loop fusion | flops 4128768 | bytes 16515076 | tf_op jit(solution)/shard_map/sub | solution.py:196
  (86 shorter events, 19.9 us)
Async XLA Ops:
  7.2 232.4 %copy-start = (f32[8,768]{1,0:T(8,128)S(1)}, f32[8,768]{1,0:T(8,128)}, u32[]{:S(2)}) copy-start(f32[8,768]{1,0:T(8,128)} %param.26) | copy-start | bytes 73732
  7.2 223.0 %reduce-scatter.2.cloned.1.call-start = ((), (), s32[]{:S(2)}) async-start(), calls=%async_computation.1 | async-start | bytes 1622016 | tf_op jit(solution)/shard_map/reduce_scatter | solution.py:152
  27.9 1.9 copy-start.4
  29.8 3.6 copy-start.2
  31.7 2.7 copy-start.1
  34.3 2.5 copy-start.19
  35.6 1.7 copy-start.5
  36.8 2.2 copy-start.7
  37.3 1.7 copy-start.10
  39.0 0.7 copy-start.9
  39.4 1.6 copy-start.16
  39.4 50.9 %copy-start.17 = (s32[8]{0:T(128)S(1)}, s32[8]{0:T(128)}, u32[]{:S(2)}) copy-start(s32[8]{0:T(128)} %param.22) | copy-start | bytes 100
  41.4 90.9 %copy-start.11 = (f32[32,12]{0,1:T(8,128)S(1)}, f32[32,12]{0,1:T(8,128)}, u32[]{:S(2)}) copy-start(f32[32,12]{0,1:T(8,128)} %param.28) | copy-start | bytes 4612
  41.4 91.8 %copy-start.13 = (f32[32,12]{0,1:T(8,128)S(1)}, f32[32,12]{0,1:T(8,128)}, u32[]{:S(2)}) copy-start(f32[32,12]{0,1:T(8,128)} %param.31) | copy-start | bytes 4612
  233.9 1.7 copy-start.6
  235.5 2.6 copy-start.8
  235.5 2.6 copy-start.18
  366.2 2.0 copy-start.3
  410.9 12.6 %copy-start.12 = (f32[8,768]{1,0:T(8,128)}, f32[8,768]{1,0:T(8,128)S(1)}, u32[]{:S(2)}) copy-start(f32[8,768]{1,0:T(8,128)S(1)} %get-tuple-element.48) | copy-start | bytes 73732
  417.0 6.5 %copy-start.14 = (f32[1153]{0:T(1024)S(1)}, f32[1153]{0:T(1024)}, u32[]{:S(2)}) copy-start(f32[1153]{0:T(1024)} %constant.45.clone.1) | copy-start | bytes 13840
  417.0 6.5 %copy-start.15 = (f32[768]{0:T(1024)S(1)}, f32[768]{0:T(1024)}, u32[]{:S(2)}) copy-start(f32[768]{0:T(1024)} %param.30) | copy-start | bytes 9220
Sparse Core Ops, SparseCore 0:
  132.5 97.6 reduce-scatter.1
where the time goes:
time: 437 us; the launch traced here: 432 us
  blocking collectives  166 us (38%)
  waiting for transfers between devices  94 us (22%)
  other arithmetic  72.5 us (17%)
  matrix products  44.6 us (10%)
  local copies, waits for them, and re-layouts  31.3 us (7%)
  between operations  24.1 us (6%)
    reduce_scatter x1, waiting for transfers between devices, local(): lax.psum_scatter(contract_first(grad_low, anchors), ('wide', 'narrow'), s...  94 us
    all_gather x1, blocking collectives, local(): lax.all_gather(own_cands, ('wide', 'narrow'), axis=0, tiled=True)  48.2 us
    psum x1, blocking collectives, local(): lax.psum((row_part, vector_grad, loss_local), ('wide', 'narrow'))  40.3 us
    psum x1, blocking collectives, local(): lax.psum(jnp.dot(ortho, matrices, precision=HIGHEST_PREC), ('wide', 'narr...  40.2 us
    psum x1, blocking collectives, local(): live_total = lax.psum(jnp.sum(live_rows), ('wide', 'narrow'))  37.3 us
    reduce_sum x9, other arithmetic, orthonormal_rows(): vector = vector - jnp.sum(vector * earlier) * earlier  28 us
    mul x2, other arithmetic, orthonormal_rows(): vector = vector * lax.rsqrt(jnp.sum(vector * vector) + EPSILON)  17.6 us
    unnamed x51, local copies, waits for them, and re-layouts  13.8 us
  transfers between devices with their start and end apart: 1, of which 1 were waited for; matrix products, arithmetic and copies ran while one was open for 1% of the time, Pallas kernels for 0%

commit v1 on v0

v1 whole, which is shorter than its diff:
```python
import functools

import jax
import jax.numpy as jnp
import numpy as np
from jax import lax
from jax.experimental import pallas as pl
from jax.experimental.pallas import tpu as pltpu
from jax.sharding import PartitionSpec as P

D = 768
HEADS = 12
HEAD_DIM = 64
BUCKETS = 32
LEN = 128
ROWS_DEV = 8
RANK = 8
TOK = ROWS_DEV * LEN
PAIRS = HEADS // 2
HALF = D // 2
FLAT = BUCKETS * HEADS
PACK = D + HALF
GROUP = 32
WIDTH = D + 128

EPSILON = 1e-06
MOMENTUM_DECAY = 0.9
CLIP_NORM = 0.01
RATE_MATRIX = 50000.0
RATE_GAIN = 4000.0
RATE_BIAS = 2000.0
RATE_SCALE = 10.0
MASKED = -float(2**30)
UNLABELLED = 2.0
F32 = jnp.float32
BF16 = jnp.bfloat16
MESH = pl.DeviceIdType.MESH


def diagonal_buckets():
    half_count = BUCKETS // 2
    exact_count = half_count // 2
    table = np.full((2 * LEN,), -1, np.int64)
    for k in range(2 * LEN):
        if k == LEN:
            continue
        relative = -k if k < LEN else 2 * LEN - k
        distance = abs(relative)
        larger = exact_count + int(
            np.log(np.maximum(distance, 1) / exact_count)
            / np.log(128.0 / exact_count)
            * (half_count - exact_count)
        )
        larger = min(larger, half_count - 1)
        table[k] = (half_count if relative > 0 else 0) + (
            distance if distance < exact_count else larger
        )
    return table


def diagonal_onehot():
    table = diagonal_buckets()
    return (table[:, None] == (np.arange(FLAT) // HEADS)[None, :]).astype(np.float32)


def head_mask():
    return (np.arange(16)[:, None] == (np.arange(FLAT) % HEADS)[None, :]).astype(np.float32)


def nn(left, right):
    return lax.dot_general(
        left, right, (((1,), (0,)), ((), ())), preferred_element_type=F32
    )


def nt(left, right):
    return lax.dot_general(
        left, right, (((1,), (1,)), ((), ())), preferred_element_type=F32
    )


def tn(left, right):
    return lax.dot_general(
        left, right, (((0,), (0,)), ((), ())), preferred_element_type=F32
    )


def parts_of(x):
    high = x.astype(BF16).astype(F32)
    rest = x - high
    middle = rest.astype(BF16).astype(F32)
    return high, middle, rest - middle


def stacked_parts(x):
    high, middle, low = parts_of(x)
    return jnp.concatenate([high, middle, low, jnp.zeros_like(x)], axis=0).astype(BF16)


def folded(y, rows):
    return y[0:rows] + y[rows : 2 * rows] + y[2 * rows : 3 * rows]


def looped(count, body, carry):
    if count == 1:
        return body(0, carry)
    return lax.fori_loop(0, count, body, carry)


def step_kernel(
    n_wide,
    n_narrow,
    proj_hbm,
    resid_hbm,
    weight_hbm,
    error_hbm,
    seg_ref,
    pad_ref,
    roles_ref,
    label_ref,
    factor_ref,
    gain_ref,
    bias_flat_ref,
    scale_ref,
    onehot_ref,
    head_mask_ref,
    ortho_ref,
    fnew_ref,
    vec_ref,
    live_ref,
    matrix_hbm,
    proj,
    resid,
    weight,
    error,
    weight_low,
    bias_table,
    key_extra,
    query_extra,
    member,
    member_t,
    probs,
    mixed_t,
    zed,
    rms_inv,
    branch,
    mixed_grad,
    matrix,
    matrix_high,
    matrix_low,
    gather,
    anchors_all,
    own_scores,
    diagonals,
    plane1,
    line1,
    plane2,
    line2,
    row_sem,
    resid_sem,
    load_sem,
    out_sem,
    gather_send,
    gather_recv,
    plane_send,
    plane_recv,
    line_send,
    line_recv,
):
    count = n_wide * n_narrow
    lines = n_wide // 2
    spots = 2 * n_narrow
    cross = n_narrow
    wide = lax.axis_index("wide")
    narrow = lax.axis_index("narrow")
    me = wide * n_narrow + narrow
    line = wide // 2
    side = wide % 2
    spot = side * n_narrow + narrow
    cell = side * (n_narrow // 2) + narrow // 2

    def spot_device(k):
        other = (spot + k) % spots
        return other, (line * 2 + other // n_narrow, other % n_narrow)

    def line_device(k):
        other = (line + k) % lines
        return other, (other * 2 + side, narrow)

    def cell_device(k):
        other = (cell + k) % cross
        return other // (n_narrow // 2), (other % (n_narrow // 2)) * 2 + narrow % 2

    sibling = (wide, narrow + 1 - 2 * (narrow % 2))

    row_copies = []
    for r in range(ROWS_DEV):
        rows = pl.ds(r * LEN, LEN)
        pltpu.make_async_copy(proj_hbm.at[:, rows, :], proj.at[:, rows, :], row_sem.at[r]).start()
    weight_copy = pltpu.make_async_copy(weight_hbm, weight, load_sem.at[0])
    weight_copy.start()
    resid_copy = pltpu.make_async_copy(resid_hbm, resid, resid_sem)
    resid_copy.start()
    error_copy = pltpu.make_async_copy(error_hbm.at[0], error, load_sem.at[1])
    error_copy.start()
    barrier = pltpu.get_barrier_semaphore()
    for k in range(1, spots):
        pl.semaphore_signal(barrier, inc=1, device_id=spot_device(k)[1], device_id_type=MESH)
    for k in range(1, lines):
        pl.semaphore_signal(barrier, inc=1, device_id=line_device(k)[1], device_id_type=MESH)

    onehot = onehot_ref[...]
    spread_bias = bias_flat_ref[...] * head_mask_ref[...]
    high, middle, low = parts_of(spread_bias)
    diag_bias = folded(
        nt(jnp.concatenate([high, middle, low], axis=0).astype(BF16), onehot), 16
    )
    for h in range(HEADS):
        wide_row = jnp.broadcast_to(diag_bias[h : h + 1, :], (LEN, 2 * LEN))
        bias_table[h] = pltpu.roll(wide_row, 0, 1, stride=1, stride_axis=0)[:, :LEN]

    code = jnp.where(pad_ref[...] == 1, seg_ref[...], 3).astype(F32)
    seg_f = seg_ref[...].astype(F32)
    fill = jnp.zeros((LEN - 16, LEN), F32)
    code_t = jnp.concatenate([code, seg_f, fill], axis=0).T
    roles_f = roles_ref[...].astype(F32)
    lane = lax.broadcasted_iota(jnp.int32, (1, LEN), 1)
    slot = lane % 32
    row_of = lax.broadcasted_iota(jnp.int32, (32, 1), 0)
    role_col = jnp.concatenate(
        [roles_f[:, 0:1], roles_f[:, 1:2], roles_f[:, 2:3], jnp.full((8, 1), 9.0, F32)], axis=0
    )
    sentence = lax.broadcasted_iota(jnp.int32, (1, LEN), 1).astype(F32)
    for r in range(ROWS_DEV):
        code_col = code_t[:, r : r + 1]
        seg_col = code_t[:, 8 + r : 9 + r]
        key_extra[r] = jnp.where(
            (sentence < 3.0) & (sentence != code_col), MASKED, 0.0
        ).astype(BF16)
        query_extra[r] = jnp.where(sentence == seg_col, 1.0, 0.0).astype(BF16)
        role_lane = jnp.where(
            slot < 8,
            roles_f[r : r + 1, 0:1],
            jnp.where(slot < 16, roles_f[r : r + 1, 1:2], roles_f[r : r + 1, 2:3]),
        )
        role_lane = jnp.where((slot < 24) & (slot % 8 == r), role_lane, 9.0)
        member_t[r * LEN : (r + 1) * LEN, :] = jnp.where(role_lane == code_col, 1.0, 0.0).astype(
            BF16
        )
        member[:, r * LEN : (r + 1) * LEN] = jnp.where(
            (role_col == code[r : r + 1, :]) & (row_of % 8 == r), 1.0, 0.0
        ).astype(BF16)
    counts = jnp.sum(member[...].astype(F32), axis=1, keepdims=True)[0:24]

    first = jnp.where(lane < HEAD_DIM, 1.0, 0.0).astype(BF16)
    second = jnp.where(lane < HEAD_DIM, 0.0, 1.0).astype(BF16)
    nothing = jnp.zeros((HEAD_DIM, LEN), BF16)

    def attend(r, carry):
        offset = pl.multiple_of(r * LEN, LEN)
        rows = pl.ds(offset, LEN)
        pltpu.make_async_copy(proj_hbm.at[:, rows, :], proj.at[:, rows, :], row_sem.at[r]).wait()
        key_more = key_extra[r]
        query_more = query_extra[r]
        for p in range(PAIRS):
            cols = slice(p * LEN, (p + 1) * LEN)
            query = proj[0, rows, cols]
            left = jnp.concatenate([proj[1, rows, cols], key_more], axis=1)
            right = jnp.concatenate(
                [
                    jnp.concatenate([query * first, query_more], axis=1),
                    jnp.concatenate([query * second, query_more], axis=1),
                ],
                axis=0,
            )
            scores = nt(left, right)
            low_probs = []
            for half in range(2):
                head = 2 * p + half
                part = scores[:, half * LEN : (half + 1) * LEN] + bias_table[head]
                part = jnp.exp(part - jnp.max(part, axis=0, keepdims=True))
                part = part * (1.0 / jnp.sum(part, axis=0, keepdims=True))
                probs[r * HEADS + head] = part
                low_probs.append(part.astype(BF16))
            value_t = proj[2, rows, cols].T
            left = jnp.concatenate(
                [
                    jnp.concatenate([value_t[:HEAD_DIM], nothing], axis=1),
                    jnp.concatenate([nothing, value_t[HEAD_DIM:]], axis=1),
                ],
                axis=0,
            )
            mixed_t[cols, rows] = nn(left, jnp.concatenate(low_probs, axis=0)).astype(BF16)
        return carry

    lax.fori_loop(0, ROWS_DEV, attend, 0)

    weight_copy.wait()
    weight_low[...] = weight[...].astype(BF16)
    resid_copy.wait()
    sums = jnp.zeros((32, D), F32)
    for c in range(4):
        rows = slice(c * 256, (c + 1) * 256)
        hidden = resid[rows, :].astype(F32) + tn(mixed_t[:, rows], weight_low[...])
        inv = lax.rsqrt(jnp.sum(hidden * hidden, axis=1, keepdims=True) * (1.0 / D) + EPSILON)
        zed_rows = hidden * inv
        zed[rows, :] = zed_rows
        rms_inv[rows, :] = inv
        high = zed_rows.astype(BF16)
        low = (zed_rows - high.astype(F32)).astype(BF16)
        picked = member[:, rows]
        sums = sums + (nn(picked, high) + nn(picked, low))
    gain = gain_ref[...]
    zed_mean = sums[0:24] / counts
    means = zed_mean * gain
    inverse = lax.rsqrt(jnp.sum(means * means, axis=1, keepdims=True) + EPSILON)
    unit = means * inverse

    same = lax.broadcasted_iota(jnp.int32, (8, 8), 0) == lax.broadcasted_iota(jnp.int32, (8, 8), 1)
    live_own = jnp.sum(
        jnp.where(same, label_ref[...].astype(F32), 0.0), axis=1, keepdims=True
    )
    wide_lane = lax.broadcasted_iota(jnp.int32, (8, D), 1)
    marked = jnp.where(
        live_own > 0.5, unit[0:8], jnp.where(wide_lane == 0, UNLABELLED, 0.0)
    )
    own_cands = unit[8:24].astype(BF16)
    gather[me, :, 0:D] = own_cands
    gather[me, :, D:PACK] = jnp.concatenate([marked[:, :HALF], marked[:, HALF:]], axis=0).astype(
        BF16
    )
    own_anchors = jnp.concatenate([marked, jnp.zeros_like(marked)], axis=0).astype(BF16)

    pl.semaphore_wait(barrier, spots + lines - 2)
    sends = []

    def send_block(block, device):
        copy = pltpu.make_async_remote_copy(
            src_ref=gather.at[block],
            dst_ref=gather.at[block],
            send_sem=gather_send.at[len(sends)],
            recv_sem=gather_recv.at[block],
            device_id=device,
            device_id_type=MESH,
        )
        copy.start()
        sends.append(copy)

    def await_block(block):
        pltpu.make_async_remote_copy(
            src_ref=gather.at[block],
            dst_ref=gather.at[block],
            send_sem=gather_send.at[0],
            recv_sem=gather_recv.at[block],
            device_id=sibling,
            device_id_type=MESH,
        ).wait_recv()

    for k in range(1, lines):
        send_block(me, line_device(k)[1])
    for k in range(lines):
        block_line, (block_wide, _) = line_device(k)
        block = block_wide * n_narrow + narrow
        if k:
            await_block(block)
        for j in range(1, cross):
            other_side, other_narrow = cell_device(j)
            send_block(block, (line * 2 + other_side, other_narrow))
        send_block(block, sibling)
    for k in range(lines):
        for j in range(1, cross):
            other_side, other_narrow = cell_device(j)
            block = ((line + k) % lines * 2 + other_side) * n_narrow + other_narrow
            await_block(block)
            send_block(block, sibling)

    error_copy.wait()
    factor_parts = stacked_parts(factor_ref[...])
    error_rows = error[...]
    error_high = error_rows.astype(BF16)
    error_low = (error_rows - error_high.astype(F32)).astype(BF16)
    row_part = folded(nt(factor_parts, error_high) + nt(factor_parts, error_low), RANK)

    for k in range(lines):
        for j in range(cross):
            other_side, other_narrow = cell_device(j)
            block = (
                ((line + k) % lines * 2 + other_side) * n_narrow
                + other_narrow
                + 1
                - 2 * (narrow % 2)
            )
            await_block(block)
    for copy in sends:
        copy.wait_send()

    blocks = count // GROUP
    temper = jnp.exp(scale_ref[...])

    def unpack(b, total):
        picked = gather[pl.ds(b * GROUP, GROUP), :, D:PACK].astype(F32)
        left = picked[:, 0:8, :].reshape(GROUP * 8, HALF)
        right = picked[:, 8:16, :].reshape(GROUP * 8, HALF)
        anchors_all[b] = jnp.concatenate([left, right], axis=1).astype(BF16)
        live = jnp.where(left[:, 0:1] < 1.5, 1.0, 0.0)
        return total + jnp.sum(live, axis=0, keepdims=True)

    live_total = looped(blocks, unpack, jnp.zeros((1, 1), F32))

    def cands_of(b):
        return gather[pl.ds(b * GROUP, GROUP), :, 0:D].reshape(GROUP * 16, D)

    first_lane = jnp.where(lax.broadcasted_iota(jnp.int32, (16, D), 1) == 0, 1.0, 0.0).astype(BF16)
    row16 = lax.broadcasted_iota(jnp.int32, (16, GROUP * 8), 0)
    lane16 = lax.broadcasted_iota(jnp.int32, (16, GROUP * 8), 1)
    per_live = 1.0 / live_total

    def columns(b, cand_grad):
        anchors = anchors_all[b]

        def part(c, state):
            top, total = state
            logits = temper * nt(cands_of(c), anchors)
            new_top = jnp.maximum(top, jnp.max(logits, axis=0, keepdims=True))
            total = total * jnp.exp(top - new_top) + jnp.sum(
                jnp.exp(logits - new_top), axis=0, keepdims=True
            )
            return new_top, total

        start = (jnp.full((1, GROUP * 8), -1e30, F32), jnp.zeros((1, GROUP * 8), F32))
        top, total = looped(blocks, part, start)
        log_total = top + jnp.log(total)
        live = jnp.where(nt(first_lane, anchors) < 1.5, per_live, 0.0)
        logits = temper * nt(own_cands, anchors)
        target = jnp.where(
            (row16 < 8) & (lane16 + b * (GROUP * 8) == row16 + me * ROWS_DEV), 1.0, 0.0
        )
        grad = (jnp.exp(logits - log_total) - target) * live
        return cand_grad + nn((temper * grad).astype(BF16), anchors)

    cand_grad = looped(blocks, columns, jnp.zeros((16, D), F32))

    def own_part(b, state):
        top, total = state
        logits = temper * nt(own_anchors, cands_of(b))
        own_scores[b] = logits
        new_top = jnp.maximum(top, jnp.max(logits, axis=1, keepdims=True))
        total = total * jnp.exp(top - new_top) + jnp.sum(
            jnp.exp(logits - new_top), axis=1, keepdims=True
        )
        return new_top, total

    start = (jnp.full((16, 1), -1e30, F32), jnp.zeros((16, 1), F32))
    top, total = looped(blocks, own_part, start)
    log_total = top + jnp.log(total)
    live16 = jnp.concatenate([live_own, jnp.zeros_like(live_own)], axis=0)
    row32 = lax.broadcasted_iota(jnp.int32, (16, GROUP * 16), 0)
    lane32 = lax.broadcasted_iota(jnp.int32, (16, GROUP * 16), 1)

    def own_grad(b, state):
        anchor_grad, positive, scale_grad = state
        logits = own_scores[b]
        target = jnp.where(
            (row32 < 8) & (lane32 + b * (GROUP * 16) == row32 + me * 2 * ROWS_DEV), 1.0, 0.0
        )
        positive = positive + jnp.sum(logits * target, axis=1, keepdims=True)
        grad = (jnp.exp(logits - log_total) - target) * (live16 * per_live)
        scale_grad = scale_grad + jnp.sum(grad * logits, axis=1, keepdims=True)
        anchor_grad = anchor_grad + nn((temper * grad).astype(BF16), cands_of(b))
        return anchor_grad, positive, scale_grad

    column = jnp.zeros((16, 1), F32)
    anchor_grad, positive, scale_grad = looped(
        blocks, own_grad, (jnp.zeros((16, D), F32), column, column)
    )
    loss_own = jnp.sum(live16 * (log_total - positive), axis=0, keepdims=True)
    scale_grad = jnp.sum(scale_grad, axis=0, keepdims=True)

    unit_grad = jnp.concatenate([anchor_grad[0:8], cand_grad], axis=0)
    mean_grad = inverse * (unit_grad - unit * jnp.sum(unit * unit_grad, axis=1, keepdims=True))
    gain_grad = jnp.sum(mean_grad * zed_mean, axis=0, keepdims=True)
    high, middle, low = parts_of(mean_grad / counts * gain)
    gap = jnp.zeros((8, D), F32)
    shares = jnp.concatenate(
        [high, gap, middle, gap, low, gap, jnp.zeros((32, D), F32)], axis=0
    ).astype(BF16)
    for c in range(4):
        rows = slice(c * 256, (c + 1) * 256)
        zed_grad = nn(member_t[rows, :], shares)
        zed_rows = zed[rows, :]
        level = jnp.sum(zed_grad * zed_rows, axis=1, keepdims=True) * (1.0 / D)
        branch[rows, :] = (rms_inv[rows, :] * (zed_grad - zed_rows * level)).astype(BF16)
    by_token = folded(nt(factor_parts, branch[...]), RANK)
    row_part = row_part + folded(nt(stacked_parts(by_token), mixed_t[...]), RANK)

    def send_to(buffers, mine, device, send_sem, recv_sem):
        copy = pltpu.make_async_remote_copy(
            src_ref=buffers.at[mine],
            dst_ref=buffers.at[mine],
            send_sem=send_sem,
            recv_sem=recv_sem.at[mine],
            device_id=device,
            device_id_type=MESH,
        )
        copy.start()
        return copy

    def await_from(buffers, other, send_sem, recv_sem):
        pltpu.make_async_remote_copy(
            src_ref=buffers.at[other],
            dst_ref=buffers.at[other],
            send_sem=send_sem,
            recv_sem=recv_sem.at[other],
            device_id=sibling,
            device_id_type=MESH,
        ).wait_recv()

    def start_sum(which, plane):
        return [
            send_to(plane, spot, spot_device(k)[1], plane_send.at[which, k], plane_recv.at[which])
            for k in range(1, spots)
        ]

    def finish_sum(which, plane, started, along):
        for k in range(1, spots):
            await_from(plane, spot_device(k)[0], plane_send.at[which, 0], plane_recv.at[which])
        total = plane[0]
        for k in range(1, spots):
            total = total + plane[k]
        along[line] = total
        second = [
            send_to(along, line, line_device(k)[1], line_send.at[which, k], line_recv.at[which])
            for k in range(1, lines)
        ]
        for k in range(1, lines):
            await_from(along, line_device(k)[0], line_send.at[which, 0], line_recv.at[which])
        total = along[0]
        for k in range(1, lines):
            total = total + along[k]
        for copy in started + second:
            copy.wait_send()
        return total

    lane8 = lax.broadcasted_iota(jnp.int32, (1, LEN), 1)
    scalars = jnp.where(lane8 == 0, loss_own, jnp.where(lane8 == 1, scale_grad, 0.0))
    extra = jnp.concatenate(
        [gain_grad[:, k * LEN : (k + 1) * LEN] for k in range(6)]
        + [scalars, jnp.zeros((1, LEN), F32)],
        axis=0,
    )
    plane1[spot, :, 0:D] = row_part
    plane1[spot, :, D:WIDTH] = extra
    started = start_sum(0, plane1)

    for b in range(3):
        rows = slice(b * 256, (b + 1) * 256)
        full = error[rows, :] + nn(mixed_t[rows, :], branch[...])
        matrix[rows, :] = full
        high = full.astype(BF16)
        matrix_high[rows, :] = high
        matrix_low[rows, :] = (full - high.astype(F32)).astype(BF16)
    matrix_copy = pltpu.make_async_copy(matrix, matrix_hbm, out_sem)
    matrix_copy.start()

    for c in range(4):
        rows = slice(c * 256, (c + 1) * 256)
        mixed_grad[rows, :] = nt(branch[rows, :], weight_low[...]).astype(BF16)
    row8 = lax.broadcasted_iota(jnp.int32, (8, 1), 0)
    for p in range(PAIRS):
        cols = slice(p * LEN, (p + 1) * LEN)

        def back(r, acc):
            offset = pl.multiple_of(r * LEN, LEN)
            rows = pl.ds(offset, LEN)
            grad = mixed_grad[rows, cols]
            right = jnp.concatenate([grad * first, grad * second], axis=0)
            prob_grad = nt(proj[2, rows, cols], right)
            prob = jnp.concatenate(
                [probs[r * HEADS + 2 * p], probs[r * HEADS + 2 * p + 1]], axis=1
            )
            product = prob * prob_grad
            return acc + (product - prob * jnp.sum(product, axis=0, keepdims=True))

        acc = lax.fori_loop(0, ROWS_DEV, back, jnp.zeros((LEN, 2 * LEN), F32))
        for half in range(2):
            padded = jnp.concatenate(
                [acc[:, half * LEN : (half + 1) * LEN], jnp.zeros((LEN, LEN), F32)], axis=1
            )
            sheared = padded[0:8]
            for a in range(1, LEN // 8):
                sheared = sheared + pltpu.roll(padded[8 * a : 8 * a + 8], 2 * LEN - 8 * a, 1)
            for bit in (1, 2, 4):
                moved = pltpu.roll(sheared, 2 * LEN - bit, 1)
                sheared = jnp.where((row8 & bit) != 0, moved, sheared)
            head = 2 * p + half
            diagonals[head : head + 1, :] = jnp.sum(sheared, axis=0, keepdims=True)
    diagonals[HEADS:16, :] = jnp.zeros((16 - HEADS, 2 * LEN), F32)
    high, middle, low = parts_of(diagonals[...])
    by_bucket = folded(
        nn(jnp.concatenate([high, middle, low], axis=0).astype(BF16), onehot_ref[...]), 16
    )
    bias_grad = jnp.sum(by_bucket * head_mask_ref[...], axis=0, keepdims=True)

    total = finish_sum(0, plane1, started, line1)
    vec_ref[0:8, :] = total[:, D:WIDTH]
    ortho = total[:, 0:D]
    rank_row = lax.broadcasted_iota(jnp.int32, (RANK, 1), 0)
    for k in range(RANK):
        vector = ortho[k : k + 1, :]
        dots = jnp.sum(ortho * vector, axis=1, keepdims=True)
        norm = lax.rsqrt(dots[k : k + 1, :] + EPSILON)
        vector = vector * norm
        ortho = jnp.where(
            rank_row > k, ortho - (dots * norm) * vector, jnp.where(rank_row == k, vector, ortho)
        )
    ortho_ref[...] = ortho
    ortho_parts = stacked_parts(ortho)
    plane2[spot, :, 0:D] = folded(
        nn(ortho_parts, matrix_high[...]) + nn(ortho_parts, matrix_low[...]), RANK
    )
    plane2[spot, :, D:WIDTH] = jnp.concatenate(
        [bias_grad[:, k * LEN : (k + 1) * LEN] for k in range(3)] + [jnp.zeros((5, LEN), F32)],
        axis=0,
    )
    started = start_sum(1, plane2)
    total = finish_sum(1, plane2, started, line2)
    fnew_ref[...] = total[:, 0:D]
    vec_ref[8:16, :] = total[:, D:WIDTH]
    live_ref[...] = live_total
    matrix_copy.wait()


def update_kernel(
    count,
    ortho_ref,
    fnew_ref,
    vec_ref,
    weight_ref,
    momentum_ref,
    matrix_ref,
    vector_ref,
    vector_mom_ref,
    weight_out,
    momentum_out,
    error_out,
    vector_out,
    vector_mom_out,
    loss_out,
    norm_out,
):
    step = pl.program_id(0)
    ortho = ortho_ref[...]
    fnew = fnew_ref[...]
    square = jnp.zeros((RANK, 1), F32)
    for k in range(RANK):
        left = jnp.sum(ortho * ortho[k : k + 1, :], axis=1, keepdims=True)
        right = jnp.sum(fnew * fnew[k : k + 1, :], axis=1, keepdims=True)
        square = square + left * right
    square = jnp.sum(square, axis=0, keepdims=True)
    vec = vec_ref[...]
    lane = lax.broadcasted_iota(jnp.int32, (1, LEN), 1)
    scale_row = jnp.where(lane == 0, vec[6:7, 1:2], 0.0)
    grad = jnp.concatenate(
        [vec[0:6], vec[8:11], scale_row, jnp.zeros((6, LEN), F32)], axis=0
    )
    square = square + jnp.sum(
        jnp.sum(grad * grad, axis=1, keepdims=True), axis=0, keepdims=True
    )
    norm = jnp.sqrt(square)
    clip = CLIP_NORM / jnp.maximum(norm, CLIP_NORM)

    @pl.when(step == 0)
    def _():
        row = lax.broadcasted_iota(jnp.int32, (16, 1), 0)
        rate = jnp.where(row < 6, RATE_GAIN, jnp.where(row < 9, RATE_BIAS, RATE_SCALE))
        mom = MOMENTUM_DECAY * vector_mom_ref[...] + clip * grad
        vector_mom_out[...] = mom
        vector_out[...] = vector_ref[...] - rate * mom
        loss_out[...] = vec[6:7, 0:1]
        norm_out[...] = norm

    rows = pl.ds(pl.multiple_of(step * 256, 256), 256)
    block = ortho_ref[:, rows]
    oh, om, ol = parts_of(block)
    fh, fm, fl = parts_of(fnew)
    pad = jnp.zeros((16, 256), F32)
    left = jnp.concatenate([oh, oh, om, om, oh, ol, pad], axis=0).astype(BF16)
    pad = jnp.zeros((16, D), F32)
    right = jnp.concatenate([fh, fm, fh, fm, fl, fh, pad], axis=0).astype(BF16)
    approx = tn(left, right)
    mom = MOMENTUM_DECAY * momentum_ref[...] + clip * approx
    momentum_out[...] = mom
    weight_out[...] = weight_ref[...] - RATE_MATRIX * mom
    error_out[0] = matrix_ref[...] - approx * (1.0 / count)


def local(
    n_wide,
    n_narrow,
    projected,
    layer_input,
    segment_ids,
    pad_mask,
    roles,
    labelled,
    out_weight,
    out_momentum,
    errors,
    factors,
    norm_gain,
    position_bias,
    log_scale,
    gain_momentum,
    bias_momentum,
    scale_momentum,
):
    count = n_wide * n_narrow
    lines = n_wide // 2
    spots = 2 * n_narrow
    blocks = count // GROUP
    sends = (lines - 1) + lines * n_narrow + lines * (n_narrow - 1)
    anywhere = pl.BlockSpec(memory_space=pl.ANY)
    vmem = pl.BlockSpec(memory_space=pltpu.VMEM)
    ortho, fnew, vec, live_total, matrix = pl.pallas_call(
        functools.partial(step_kernel, n_wide, n_narrow),
        out_shape=(
            jax.ShapeDtypeStruct((RANK, D), F32),
            jax.ShapeDtypeStruct((RANK, D), F32),
            jax.ShapeDtypeStruct((16, LEN), F32),
            jax.ShapeDtypeStruct((1, 1), F32),
            jax.ShapeDtypeStruct((D, D), F32),
        ),
        in_specs=[anywhere] * 4 + [vmem] * 10,
        out_specs=(vmem, vmem, vmem, vmem, anywhere),
        scratch_shapes=[
            pltpu.VMEM((3, TOK, D), BF16),
            pltpu.VMEM((TOK, D), BF16),
            pltpu.VMEM((D, D), F32),
            pltpu.VMEM((D, D), F32),
            pltpu.VMEM((D, D), BF16),
            pltpu.VMEM((HEADS, LEN, LEN), F32),
            pltpu.VMEM((ROWS_DEV, LEN, LEN), BF16),
            pltpu.VMEM((ROWS_DEV, LEN, LEN), BF16),
            pltpu.VMEM((32, TOK), BF16),
            pltpu.VMEM((TOK, LEN), BF16),
            pltpu.VMEM((ROWS_DEV * HEADS, LEN, LEN), F32),
            pltpu.VMEM((D, TOK), BF16),
            pltpu.VMEM((TOK, D), F32),
            pltpu.VMEM((TOK, 1), F32),
            pltpu.VMEM((TOK, D), BF16),
            pltpu.VMEM((TOK, D), BF16),
            pltpu.VMEM((D, D), F32),
            pltpu.VMEM((D, D), BF16),
            pltpu.VMEM((D, D), BF16),
            pltpu.VMEM((count, 16, PACK), BF16),
            pltpu.VMEM((blocks, GROUP * 8, D), BF16),
            pltpu.VMEM((blocks, 16, GROUP * 16), F32),
            pltpu.VMEM((16, 2 * LEN), F32),
            pltpu.VMEM((spots, RANK, WIDTH), F32),
            pltpu.VMEM((lines, RANK, WIDTH), F32),
            pltpu.VMEM((spots, RANK, WIDTH), F32),
            pltpu.VMEM((lines, RANK, WIDTH), F32),
            pltpu.SemaphoreType.DMA((ROWS_DEV,)),
            pltpu.SemaphoreType.DMA,
            pltpu.SemaphoreType.DMA((2,)),
            pltpu.SemaphoreType.DMA,
            pltpu.SemaphoreType.DMA((sends,)),
            pltpu.SemaphoreType.DMA((count,)),
            pltpu.SemaphoreType.DMA((2, spots)),
            pltpu.SemaphoreType.DMA((2, spots)),
            pltpu.SemaphoreType.DMA((2, lines)),
            pltpu.SemaphoreType.DMA((2, lines)),
        ],
        compiler_params=pltpu.CompilerParams(
            collective_id=0, has_side_effects=True, vmem_limit_bytes=60 * 2**20
        ),
        name="step",
    )(
        projected,
        layer_input,
        out_weight,
        errors,
        segment_ids.reshape(ROWS_DEV, LEN),
        pad_mask.reshape(ROWS_DEV, LEN),
        roles,
        labelled.reshape(1, ROWS_DEV),
        factors,
        norm_gain.reshape(1, D),
        position_bias.reshape(1, FLAT),
        log_scale.reshape(1, 1),
        jnp.asarray(diagonal_onehot(), BF16),
        jnp.asarray(head_mask()),
    )
    padding = jnp.zeros((16 * LEN - D - FLAT - 1,), F32)
    vector = jnp.concatenate([norm_gain, position_bias.reshape(-1), log_scale, padding])
    vector_mom = jnp.concatenate([gain_momentum, bias_momentum.reshape(-1), scale_momentum, padding])
    whole = lambda *shape: pl.BlockSpec(shape, lambda i: (0,) * len(shape))
    rows = pl.BlockSpec((256, D), lambda i: (i, 0))
    outs = pl.pallas_call(
        functools.partial(update_kernel, count),
        grid=(3,),
        out_shape=(
            jax.ShapeDtypeStruct((D, D), F32),
            jax.ShapeDtypeStruct((D, D), F32),
            jax.ShapeDtypeStruct((1, D, D), F32),
            jax.ShapeDtypeStruct((16, LEN), F32),
            jax.ShapeDtypeStruct((16, LEN), F32),
            jax.ShapeDtypeStruct((1, 1), F32),
            jax.ShapeDtypeStruct((1, 1), F32),
        ),
        in_specs=[
            whole(RANK, D),
            whole(RANK, D),
            whole(16, LEN),
            rows,
            rows,
            rows,
            whole(16, LEN),
            whole(16, LEN),
        ],
        out_specs=(
            rows,
            rows,
            pl.BlockSpec((1, 256, D), lambda i: (0, i, 0)),
            whole(16, LEN),
            whole(16, LEN),
            whole(1, 1),
            whole(1, 1),
        ),
        name="update",
    )(
        ortho,
        fnew,
        vec,
        out_weight,
        out_momentum,
        matrix,
        vector.reshape(16, LEN),
        vector_mom.reshape(16, LEN),
    )
    weight_new, weight_mom, errors_new, vec_new, vec_mom, loss, norm = outs
    size = D + FLAT + 1
    return (
        weight_new,
        weight_mom,
        errors_new,
        fnew,
        vec_new.reshape(-1)[:size],
        vec_mom.reshape(-1)[:size],
        loss.reshape(1),
        live_total.reshape(1),
        norm.reshape(1),
    )


def solution(mesh):
    both = ("wide", "narrow")
    in_specs = (
        P(None, both, None),
        P(both, None),
        P(both),
        P(both),
        P(both, None),
        P(both),
        P(),
        P(),
        P(both, None, None),
        P(),
        P(),
        P(),
        P(),
        P(),
        P(),
        P(),
    )
    out_specs = (P(), P(), P(both, None, None), P(), P(), P(), P(), P(), P())
    return jax.shard_map(
        functools.partial(local, mesh.shape["wide"], mesh.shape["narrow"]),
        mesh=mesh,
        in_specs=in_specs,
        out_specs=out_specs,
        check_vma=False,
    )
```

time: 437 us -> 85.6 us (0.20)
  blocking collectives: 166 us -> 0 us
  waiting for transfers between devices: 94 us -> 0 us
  Pallas kernels: 0 us -> 75.2 us
  other arithmetic: 72.5 us -> 0 us
  matrix products: 44.6 us -> 0 us
  local copies, waits for them, and re-layouts: 31.3 us -> 6.32 us
  between operations: 24.1 us -> 3.74 us
    psum x3 -> x0, blocking collectives: 118 us -> none  [the longest x1 40.3 us: local(): lax.psum((row_part, vector_grad, loss_local), ('wide', 'narrow'))]
    reduce_scatter x1 -> x0, waiting for transfers between devices: 94 us -> none  [local(): lax.psum_scatter(contract_first(grad_low, anchors), ('wide', 'narrow'), s...]
    pallas_call x0 -> x2, Pallas kernels: none -> 75.2 us  [the longest x1 67.1 us: local(): pl.pallas_call(functools.partial(step_kernel, n_wide, n_narrow), out_shap...]
    all_gather x1 -> x0, blocking collectives: 48.2 us -> none  [local(): lax.all_gather(own_cands, ('wide', 'narrow'), axis=0, tiled=True)]
    reduce_sum x22 -> x0, other arithmetic: 42.8 us -> none  [the longest x9 28 us: orthonormal_rows(): vector = vector - jnp.sum(vector * earlier) * earlier]
    dot_general x18 -> x0, matrix products: 36.1 us -> none  [the longest x1 7.68 us: local(): jnp.einsum('rihd,rjhd->rhij', mixed_grad, values, preferred_element_type=...]
    mul x4 -> x0, other arithmetic: 18.1 us -> none  [the longest x2 17.6 us: orthonormal_rows(): vector = vector * lax.rsqrt(jnp.sum(vector * vector) + EPSILON)]
    unnamed x51 -> x12, local copies, waits for them, and re-layouts: 13.8 us -> 2.84 us
  transfers between devices with their start and end apart: 1 -> 0, of which waited for: 1 -> 0; matrix products, arithmetic and copies ran while one was open for 1% -> 0% of each run, Pallas kernels for 0% -> 0%
where the time goes in v1:
time: 85.6 us; the launch traced here: 85.3 us
  Pallas kernels  75.2 us (88%)
  local copies, waits for them, and re-layouts  6.32 us (7%)
  between operations  3.74 us (4%)
    pallas_call x1, Pallas kernels, local(): pl.pallas_call(functools.partial(step_kernel, n_wide, n_narrow), out_shap...  67.1 us
    pallas_call x1, Pallas kernels, local(): pl.pallas_call(functools.partial(update_kernel, count), grid=(3,), out_sh...  8.08 us
    unnamed x12, local copies, waits for them, and re-layouts  2.84 us

profile of v1, /device:TPU:0, one launch (start us, length us, event | category | flops | bytes accessed | tf_op | source)
XLA Modules:
  0.0 85.3 jit_solution(9860118590644097376)
XLA Ops:
  0.6 0.8 copy.29
  1.4 0.7 reshape.67.bias_flat_ref
  2.7 1.4 %copy.30.roles_ref = s32[8,3]{1,0:T(8,128)} copy(s32[8,3]{0,1:T(4,128)} %param.22) | data formatting | bytes 192 | tf_op args[4]
  4.1 1.3 %reshape.66.gain_ref = f32[1,768]{1,0:T(1,128)} reshape(f32[768]{0:T(1024)} %param.28) | data formatting | bytes 6144 | tf_op jit(solution)/shard_map/reshape | solution.py:788
  5.4 0.0 copy-start.1
  5.4 0.0 copy-start.2
  5.4 0.0 copy-start.3
  5.4 67.1 %step.1 = (f32[8,768]{1,0:T(8,128)}, f32[8,768]{1,0:T(8,128)}, f32[16,128]{1,0:T(8,128)}, f32[1,1]{1,0:T(1,128)}, f32[768,768]{1,0:T(8,128)}) custom-call(bf16[3,1024,768]{2,1,0:T(8,128)(2,1)} %proj_hbm.1, bf16[1024,768]{1,0:T(8,128)(2,1)} %resid_hbm.1, f32[768,768]{1,0:T(8,128)} %weight_ref.1, f32[1,768,768]{2,1,0:T(8,128)} %error_hbm.1, ...), custom_call_target="tpu_custom_call" | custom-call | tf_op jit(solution)/shard_map/step/pallas_call | solution.py:724
  72.5 0.1 reshape.69
  72.6 0.0 copy-done.1
  72.6 0.7 concatenate.6
  73.3 0.0 copy-done.2
  73.3 0.1 copy.32
  73.4 0.1 reshape.71
  74.1 0.0 copy-done.3
  74.1 0.7 concatenate.7
  74.8 0.0 copy-start
  74.8 8.1 %update.1 = (f32[768,768]{1,0:T(8,128)}, f32[768,768]{1,0:T(8,128)}, f32[1,768,768]{2,1,0:T(8,128)}, f32[16,128]{1,0:T(8,128)}, f32[16,128]{1,0:T(8,128)}, /*index=5*/f32[1,1]{1,0:T(1,128)}, f32[1,1]{1,0:T(1,128)}) custom-call(f32[8,768]{1,0:T(8,128)} %get-tuple-element.21.ortho_ref, f32[8,768]{1,0:T(8,128)} %get-tuple-element.45.fnew_ref, ...), custom_call_target="tpu_custom_call" | custom-call | tf_op jit(solution)/shard_map/update/pallas_call | solution.py:799
  82.9 0.0 copy-done
  82.9 0.6 copy.37
  (1 shorter events, 0.0 us)
Async XLA Ops:
  5.4 67.2 %copy-start.1 = (f32[768]{0:T(1024)S(1)}, f32[768]{0:T(1024)}, u32[]{:S(2)}) copy-start(f32[768]{0:T(1024)} %param.28) | copy-start | bytes 9220
  5.4 67.9 %copy-start.2 = (f32[32,12]{0,1:T(8,128)S(1)}, f32[32,12]{0,1:T(8,128)}, u32[]{:S(2)}) copy-start(f32[32,12]{0,1:T(8,128)} %param.32) | copy-start | bytes 4612
  5.4 68.8 %copy-start.3 = (f32[768]{0:T(1024)S(1)}, f32[768]{0:T(1024)}, u32[]{:S(2)}) copy-start(f32[768]{0:T(1024)} %param.31) | copy-start | bytes 9220
  74.8 8.1 %copy-start = (f32[8,768]{1,0:T(8,128)S(1)}, f32[8,768]{1,0:T(8,128)}, u32[]{:S(2)}) copy-start(f32[8,768]{1,0:T(8,128)} %get-tuple-element.45.fnew_ref) | copy-start | bytes 73732

commit v2 on v1

--- a/solution.py
+++ b/solution.py
@@ -58,9 +58,13 @@
     return table
 
 
-def diagonal_onehot():
-    table = diagonal_buckets()
-    return (table[:, None] == (np.arange(FLAT) // HEADS)[None, :]).astype(np.float32)
+def diagonal_onehot(width):
+    spread = np.arange(width) // (width // BUCKETS)
+    return (diagonal_buckets()[:, None] == spread[None, :]).astype(np.float32)
+
+
+def bucket_spread():
+    return (np.arange(BUCKETS)[:, None] == (np.arange(FLAT) // HEADS)[None, :]).astype(np.float32)
 
 
 def head_mask():
@@ -114,21 +118,39 @@
     resid_hbm,
     weight_hbm,
     error_hbm,
+    seg_hbm,
+    pad_hbm,
+    roles_hbm,
+    label_hbm,
+    factor_hbm,
+    gain_hbm,
+    gain_mom_hbm,
+    bias_hbm,
+    bias_mom_hbm,
+    scale_hbm,
+    scale_mom_hbm,
+    onehot_hbm,
+    spread_hbm,
+    diagonal_hbm,
+    head_mask_hbm,
+    small_ref,
+    matrix_hbm,
     seg_ref,
     pad_ref,
     roles_ref,
     label_ref,
     factor_ref,
     gain_ref,
-    bias_flat_ref,
+    gain_mom_ref,
+    bias_ref,
+    bias_mom_ref,
     scale_ref,
+    scale_mom_ref,
     onehot_ref,
+    spread_ref,
+    diagonal_ref,
     head_mask_ref,
-    ortho_ref,
-    fnew_ref,
-    vec_ref,
-    live_ref,
-    matrix_hbm,
+    small_sem,
     proj,
     resid,
     weight,
@@ -140,11 +162,13 @@
     member,
     member_t,
     probs,
+    score_rows,
+    prob_rows,
     mixed_t,
     zed,
+    zed_high,
+    zed_low,
     rms_inv,
-    branch,
-    mixed_grad,
     matrix,
     matrix_high,
     matrix_low,
@@ -193,7 +217,30 @@
 
     sibling = (wide, narrow + 1 - 2 * (narrow % 2))
 
-    row_copies = []
+    small_copies = [
+        pltpu.make_async_copy(source, target, small_sem.at[k])
+        for k, (source, target) in enumerate(
+            (
+                (seg_hbm, seg_ref),
+                (pad_hbm, pad_ref),
+                (roles_hbm, roles_ref),
+                (label_hbm, label_ref),
+                (factor_hbm, factor_ref),
+                (gain_hbm, gain_ref),
+                (gain_mom_hbm, gain_mom_ref),
+                (bias_hbm, bias_ref),
+                (bias_mom_hbm, bias_mom_ref),
+                (scale_hbm, scale_ref),
+                (scale_mom_hbm, scale_mom_ref),
+                (onehot_hbm, onehot_ref),
+                (spread_hbm, spread_ref),
+                (diagonal_hbm, diagonal_ref),
+                (head_mask_hbm, head_mask_ref),
+            )
+        )
+    ]
+    for copy in small_copies:
+        copy.start()
     for r in range(ROWS_DEV):
         rows = pl.ds(r * LEN, LEN)
         pltpu.make_async_copy(proj_hbm.at[:, rows, :], proj.at[:, rows, :], row_sem.at[r]).start()
@@ -209,15 +256,25 @@
     for k in range(1, lines):
         pl.semaphore_signal(barrier, inc=1, device_id=line_device(k)[1], device_id_type=MESH)
 
-    onehot = onehot_ref[...]
-    spread_bias = bias_flat_ref[...] * head_mask_ref[...]
-    high, middle, low = parts_of(spread_bias)
+    for copy in small_copies:
+        copy.wait()
+    high, middle, low = parts_of(bias_ref[...])
+    gap = jnp.zeros((4, BUCKETS), F32)
     diag_bias = folded(
-        nt(jnp.concatenate([high, middle, low], axis=0).astype(BF16), onehot), 16
-    )
+        nt(
+            jnp.concatenate([high, gap, middle, gap, low, gap], axis=0).astype(BF16),
+            diagonal_ref[...],
+        ),
+        16,
+    )
+    row8 = lax.broadcasted_iota(jnp.int32, (8, 1), 0)
     for h in range(HEADS):
-        wide_row = jnp.broadcast_to(diag_bias[h : h + 1, :], (LEN, 2 * LEN))
-        bias_table[h] = pltpu.roll(wide_row, 0, 1, stride=1, stride_axis=0)[:, :LEN]
+        sheared = jnp.broadcast_to(diag_bias[h : h + 1, :], (8, 2 * LEN))
+        for bit in (1, 2, 4):
+            sheared = jnp.where((row8 & bit) != 0, pltpu.roll(sheared, bit, 1), sheared)
+        bias_table[h, 0:8, :] = sheared[:, :LEN]
+        for a in range(1, LEN // 8):
+            bias_table[h, 8 * a : 8 * a + 8, :] = pltpu.roll(sheared, 8 * a, 1)[:, :LEN]
 
     code = jnp.where(pad_ref[...] == 1, seg_ref[...], 3).astype(F32)
     seg_f = seg_ref[...].astype(F32)
@@ -227,8 +284,13 @@
     lane = lax.broadcasted_iota(jnp.int32, (1, LEN), 1)
     slot = lane % 32
     row_of = lax.broadcasted_iota(jnp.int32, (32, 1), 0)
+    same = lax.broadcasted_iota(jnp.int32, (8, 8), 0) == lax.broadcasted_iota(jnp.int32, (8, 8), 1)
+
+    def column_of(row):
+        return jnp.sum(jnp.where(same, row, 0.0), axis=1, keepdims=True)
+
     role_col = jnp.concatenate(
-        [roles_f[:, 0:1], roles_f[:, 1:2], roles_f[:, 2:3], jnp.full((8, 1), 9.0, F32)], axis=0
+        [column_of(roles_f[k : k + 1, :]) for k in range(3)] + [jnp.full((8, 1), 9.0, F32)], axis=0
     )
     sentence = lax.broadcasted_iota(jnp.int32, (1, LEN), 1).astype(F32)
     for r in range(ROWS_DEV):
@@ -240,8 +302,8 @@
         query_extra[r] = jnp.where(sentence == seg_col, 1.0, 0.0).astype(BF16)
         role_lane = jnp.where(
             slot < 8,
-            roles_f[r : r + 1, 0:1],
-            jnp.where(slot < 16, roles_f[r : r + 1, 1:2], roles_f[r : r + 1, 2:3]),
+            roles_f[0:1, r : r + 1],
+            jnp.where(slot < 16, roles_f[1:2, r : r + 1], roles_f[2:3, r : r + 1]),
         )
         role_lane = jnp.where((slot < 24) & (slot % 8 == r), role_lane, 9.0)
         member_t[r * LEN : (r + 1) * LEN, :] = jnp.where(role_lane == code_col, 1.0, 0.0).astype(
@@ -256,70 +318,105 @@
     second = jnp.where(lane < HEAD_DIM, 0.0, 1.0).astype(BF16)
     nothing = jnp.zeros((HEAD_DIM, LEN), BF16)
 
-    def attend(r, carry):
-        offset = pl.multiple_of(r * LEN, LEN)
-        rows = pl.ds(offset, LEN)
+    def rows_of(r):
+        return pl.ds(r * LEN if isinstance(r, int) else pl.multiple_of(r * LEN, LEN), LEN)
+
+    def arrive(r):
+        rows = rows_of(r)
         pltpu.make_async_copy(proj_hbm.at[:, rows, :], proj.at[:, rows, :], row_sem.at[r]).wait()
-        key_more = key_extra[r]
+
+    def score(r, p, k):
+        rows = rows_of(r)
+        cols = slice(p * LEN, (p + 1) * LEN)
+        query = proj[0, rows, cols]
         query_more = query_extra[r]
+        left = jnp.concatenate([proj[1, rows, cols], key_extra[r]], axis=1)
+        right = jnp.concatenate(
+            [
+                jnp.concatenate([query * first, query_more], axis=1),
+                jnp.concatenate([query * second, query_more], axis=1),
+            ],
+            axis=0,
+        )
+        score_rows[k, p] = nt(left, right)
+
+    def soften(r, p, k):
+        for half in range(2):
+            head = 2 * p + half
+            part = score_rows[k, p, :, half * LEN : (half + 1) * LEN] + bias_table[head]
+            part = jnp.exp(part - jnp.max(part, axis=0, keepdims=True))
+            part = part * (1.0 / jnp.sum(part, axis=0, keepdims=True))
+            probs[r * HEADS + head] = part
+            prob_rows[k, p, half * LEN : (half + 1) * LEN, :] = part.astype(BF16)
+
+    def mix(r, p, k):
+        rows = rows_of(r)
+        cols = slice(p * LEN, (p + 1) * LEN)
+        value_t = proj[2, rows, cols].T
+        left = jnp.concatenate(
+            [
+                jnp.concatenate([value_t[:HEAD_DIM], nothing], axis=1),
+                jnp.concatenate([nothing, value_t[HEAD_DIM:]], axis=1),
+            ],
+            axis=0,
+        )
+        mixed_t[cols, rows] = nn(left, prob_rows[k, p]).astype(BF16)
+
+    arrive(0)
+    for p in range(PAIRS):
+        score(0, p, 0)
+    arrive(1)
+    for p in range(PAIRS):
+        score(1, p, 1)
+        soften(0, p, 0)
+
+    def attend(i, carry):
+        r = 2 * i + 2
+        arrive(r)
         for p in range(PAIRS):
-            cols = slice(p * LEN, (p + 1) * LEN)
-            query = proj[0, rows, cols]
-            left = jnp.concatenate([proj[1, rows, cols], key_more], axis=1)
-            right = jnp.concatenate(
-                [
-                    jnp.concatenate([query * first, query_more], axis=1),
-                    jnp.concatenate([query * second, query_more], axis=1),
-                ],
-                axis=0,
-            )
-            scores = nt(left, right)
-            low_probs = []
-            for half in range(2):
-                head = 2 * p + half
-                part = scores[:, half * LEN : (half + 1) * LEN] + bias_table[head]
-                part = jnp.exp(part - jnp.max(part, axis=0, keepdims=True))
-                part = part * (1.0 / jnp.sum(part, axis=0, keepdims=True))
-                probs[r * HEADS + head] = part
-                low_probs.append(part.astype(BF16))
-            value_t = proj[2, rows, cols].T
-            left = jnp.concatenate(
-                [
-                    jnp.concatenate([value_t[:HEAD_DIM], nothing], axis=1),
-                    jnp.concatenate([nothing, value_t[HEAD_DIM:]], axis=1),
-                ],
-                axis=0,
-            )
-            mixed_t[cols, rows] = nn(left, jnp.concatenate(low_probs, axis=0)).astype(BF16)
+            score(r, p, 0)
+            mix(r - 2, p, 0)
+            soften(r - 1, p, 1)
+        arrive(r + 1)
+        for p in range(PAIRS):
+            score(r + 1, p, 1)
+            mix(r - 1, p, 1)
+            soften(r, p, 0)
         return carry
 
-    lax.fori_loop(0, ROWS_DEV, attend, 0)
+    lax.fori_loop(0, ROWS_DEV // 2 - 1, attend, 0)
+    for p in range(PAIRS):
+        mix(ROWS_DEV - 2, p, 0)
+        soften(ROWS_DEV - 1, p, 1)
+    for p in range(PAIRS):
+        mix(ROWS_DEV - 1, p, 1)
 
     weight_copy.wait()
     weight_low[...] = weight[...].astype(BF16)
     resid_copy.wait()
-    sums = jnp.zeros((32, D), F32)
     for c in range(4):
         rows = slice(c * 256, (c + 1) * 256)
-        hidden = resid[rows, :].astype(F32) + tn(mixed_t[:, rows], weight_low[...])
+        zed[rows, :] = resid[rows, :].astype(F32) + tn(mixed_t[:, rows], weight_low[...])
+
+    for b in range(TOK // 32):
+        rows = slice(b * 32, (b + 1) * 32)
+        hidden = zed[rows, :]
         inv = lax.rsqrt(jnp.sum(hidden * hidden, axis=1, keepdims=True) * (1.0 / D) + EPSILON)
-        zed_rows = hidden * inv
-        zed[rows, :] = zed_rows
+        hidden = hidden * inv
+        zed[rows, :] = hidden
         rms_inv[rows, :] = inv
-        high = zed_rows.astype(BF16)
-        low = (zed_rows - high.astype(F32)).astype(BF16)
-        picked = member[:, rows]
-        sums = sums + (nn(picked, high) + nn(picked, low))
-    gain = gain_ref[...]
+        high = hidden.astype(BF16)
+        zed_high[rows, :] = high
+        zed_low[rows, :] = (hidden - high.astype(F32)).astype(BF16)
+    sums = nn(member[...], zed_high[...]) + nn(member[...], zed_low[...])
+    gain_rows = gain_ref[...]
+    gain = jnp.concatenate([gain_rows[k : k + 1, :] for k in range(6)], axis=1)
     zed_mean = sums[0:24] / counts
     means = zed_mean * gain
     inverse = lax.rsqrt(jnp.sum(means * means, axis=1, keepdims=True) + EPSILON)
     unit = means * inverse
 
-    same = lax.broadcasted_iota(jnp.int32, (8, 8), 0) == lax.broadcasted_iota(jnp.int32, (8, 8), 1)
-    live_own = jnp.sum(
-        jnp.where(same, label_ref[...].astype(F32), 0.0), axis=1, keepdims=True
-    )
+    live_own = column_of(label_ref[...].astype(F32))
     wide_lane = lax.broadcasted_iota(jnp.int32, (8, D), 1)
     marked = jnp.where(
         live_own > 0.5, unit[0:8], jnp.where(wide_lane == 0, UNLABELLED, 0.0)
@@ -381,6 +478,28 @@
     error_low = (error_rows - error_high.astype(F32)).astype(BF16)
     row_part = folded(nt(factor_parts, error_high) + nt(factor_parts, error_low), RANK)
 
+    def flat_bias(x):
+        high, middle, low = parts_of(x)
+        spread = folded(
+            nn(
+                jnp.concatenate([high, gap, middle, gap, low, gap], axis=0).astype(BF16),
+                spread_ref[...],
+            ),
+            16,
+        )
+        return jnp.sum(spread * head_mask_ref[...], axis=0, keepdims=True)
+
+    def packed(gain_part, bias_part, scale_part):
+        return jnp.concatenate(
+            [gain_part]
+            + [bias_part[:, k * LEN : (k + 1) * LEN] for k in range(3)]
+            + [jnp.where(lane == 0, scale_part, 0.0), jnp.zeros((6, LEN), F32)],
+            axis=0,
+        )
+
+    small_ref[16:32, LEN : 2 * LEN] = packed(gain_rows, flat_bias(bias_ref[...]), scale_ref[...])
+    small_ref[16:32, 2 * LEN : 3 * LEN] = packed(gain_mom_ref[...], flat_bias(bias_mom_ref[...]), scale_mom_ref[...])
+
     for k in range(lines):
         for j in range(cross):
             other_side, other_narrow = cell_device(j)
@@ -476,13 +595,14 @@
     loss_own = jnp.sum(live16 * (log_total - positive), axis=0, keepdims=True)
     scale_grad = jnp.sum(scale_grad, axis=0, keepdims=True)
 
+    branch, mixed_grad = zed_high, zed_low
     unit_grad = jnp.concatenate([anchor_grad[0:8], cand_grad], axis=0)
     mean_grad = inverse * (unit_grad - unit * jnp.sum(unit * unit_grad, axis=1, keepdims=True))
     gain_grad = jnp.sum(mean_grad * zed_mean, axis=0, keepdims=True)
     high, middle, low = parts_of(mean_grad / counts * gain)
-    gap = jnp.zeros((8, D), F32)
+    wide_gap = jnp.zeros((8, D), F32)
     shares = jnp.concatenate(
-        [high, gap, middle, gap, low, gap, jnp.zeros((32, D), F32)], axis=0
+        [high, wide_gap, middle, wide_gap, low, wide_gap, jnp.zeros((32, D), F32)], axis=0
     ).astype(BF16)
     for c in range(4):
         rows = slice(c * 256, (c + 1) * 256)
@@ -541,8 +661,7 @@
             copy.wait_send()
         return total
 
-    lane8 = lax.broadcasted_iota(jnp.int32, (1, LEN), 1)
-    scalars = jnp.where(lane8 == 0, loss_own, jnp.where(lane8 == 1, scale_grad, 0.0))
+    scalars = jnp.where(lane == 0, loss_own, jnp.where(lane == 1, scale_grad, 0.0))
     extra = jnp.concatenate(
         [gain_grad[:, k * LEN : (k + 1) * LEN] for k in range(6)]
         + [scalars, jnp.zeros((1, LEN), F32)],
@@ -565,7 +684,6 @@
     for c in range(4):
         rows = slice(c * 256, (c + 1) * 256)
         mixed_grad[rows, :] = nt(branch[rows, :], weight_low[...]).astype(BF16)
-    row8 = lax.broadcasted_iota(jnp.int32, (8, 1), 0)
     for p in range(PAIRS):
         cols = slice(p * LEN, (p + 1) * LEN)
 
@@ -581,7 +699,7 @@
             product = prob * prob_grad
             return acc + (product - prob * jnp.sum(product, axis=0, keepdims=True))
 
-        acc = lax.fori_loop(0, ROWS_DEV, back, jnp.zeros((LEN, 2 * LEN), F32))
+        acc = lax.fori_loop(0, ROWS_DEV, back, jnp.zeros((LEN, 2 * LEN), F32), unroll=True)
         for half in range(2):
             padded = jnp.concatenate(
                 [acc[:, half * LEN : (half + 1) * LEN], jnp.zeros((LEN, LEN), F32)], axis=1
@@ -602,7 +720,7 @@
     bias_grad = jnp.sum(by_bucket * head_mask_ref[...], axis=0, keepdims=True)
 
     total = finish_sum(0, plane1, started, line1)
-    vec_ref[0:8, :] = total[:, D:WIDTH]
+    small_ref[16:24, 0:LEN] = total[:, D:WIDTH]
     ortho = total[:, 0:D]
     rank_row = lax.broadcasted_iota(jnp.int32, (RANK, 1), 0)
     for k in range(RANK):
@@ -613,7 +731,7 @@
         ortho = jnp.where(
             rank_row > k, ortho - (dots * norm) * vector, jnp.where(rank_row == k, vector, ortho)
         )
-    ortho_ref[...] = ortho
+    small_ref[0:8, :] = ortho
     ortho_parts = stacked_parts(ortho)
     plane2[spot, :, 0:D] = folded(
         nn(ortho_parts, matrix_high[...]) + nn(ortho_parts, matrix_low[...]), RANK
@@ -624,22 +742,19 @@
     )
     started = start_sum(1, plane2)
     total = finish_sum(1, plane2, started, line2)
-    fnew_ref[...] = total[:, 0:D]
-    vec_ref[8:16, :] = total[:, D:WIDTH]
-    live_ref[...] = live_total
+    small_ref[8:16, :] = total[:, 0:D]
+    small_ref[24:32, 0:LEN] = total[:, D:WIDTH]
+    small_ref[16:32, 3 * LEN : 4 * LEN] = jnp.broadcast_to(live_total, (16, LEN))
+    small_ref[16:32, 4 * LEN : D] = jnp.zeros((16, D - 4 * LEN), F32)
     matrix_copy.wait()
 
 
 def update_kernel(
     count,
-    ortho_ref,
-    fnew_ref,
-    vec_ref,
+    small_ref,
+    matrix_ref,
     weight_ref,
     momentum_ref,
-    matrix_ref,
-    vector_ref,
-    vector_mom_ref,
     weight_out,
     momentum_out,
     error_out,
@@ -647,17 +762,22 @@
     vector_mom_out,
     loss_out,
     norm_out,
+    fnew_out,
+    live_out,
+    matrix,
+    weight,
+    momentum,
+    store_sem,
 ):
-    step = pl.program_id(0)
-    ortho = ortho_ref[...]
-    fnew = fnew_ref[...]
+    ortho = small_ref[0:8, :]
+    fnew = small_ref[8:16, :]
     square = jnp.zeros((RANK, 1), F32)
     for k in range(RANK):
         left = jnp.sum(ortho * ortho[k : k + 1, :], axis=1, keepdims=True)
         right = jnp.sum(fnew * fnew[k : k + 1, :], axis=1, keepdims=True)
         square = square + left * right
     square = jnp.sum(square, axis=0, keepdims=True)
-    vec = vec_ref[...]
+    vec = small_ref[16:32, 0:LEN]
     lane = lax.broadcasted_iota(jnp.int32, (1, LEN), 1)
     scale_row = jnp.where(lane == 0, vec[6:7, 1:2], 0.0)
     grad = jnp.concatenate(
@@ -669,29 +789,40 @@
     norm = jnp.sqrt(square)
     clip = CLIP_NORM / jnp.maximum(norm, CLIP_NORM)
 
-    @pl.when(step == 0)
-    def _():
-        row = lax.broadcasted_iota(jnp.int32, (16, 1), 0)
-        rate = jnp.where(row < 6, RATE_GAIN, jnp.where(row < 9, RATE_BIAS, RATE_SCALE))
-        mom = MOMENTUM_DECAY * vector_mom_ref[...] + clip * grad
-        vector_mom_out[...] = mom
-        vector_out[...] = vector_ref[...] - rate * mom
-        loss_out[...] = vec[6:7, 0:1]
-        norm_out[...] = norm
-
-    rows = pl.ds(pl.multiple_of(step * 256, 256), 256)
-    block = ortho_ref[:, rows]
-    oh, om, ol = parts_of(block)
+    oh, om, ol = parts_of(ortho)
     fh, fm, fl = parts_of(fnew)
-    pad = jnp.zeros((16, 256), F32)
+    pad = jnp.zeros((16, D), F32)
     left = jnp.concatenate([oh, oh, om, om, oh, ol, pad], axis=0).astype(BF16)
-    pad = jnp.zeros((16, D), F32)
     right = jnp.concatenate([fh, fm, fh, fm, fl, fh, pad], axis=0).astype(BF16)
-    approx = tn(left, right)
-    mom = MOMENTUM_DECAY * momentum_ref[...] + clip * approx
-    momentum_out[...] = mom
-    weight_out[...] = weight_ref[...] - RATE_MATRIX * mom
-    error_out[0] = matrix_ref[...] - approx * (1.0 / count)
+    copies = []
+
+    def send_out(source, target, rows, sem):
+        copy = pltpu.make_async_copy(source.at[rows, :], target.at[rows, :], sem)
+        copy.start()
+        copies.append(copy)
+
+    for b in range(3):
+        rows = slice(b * 256, (b + 1) * 256)
+        approx = tn(left[:, rows], right)
+        mom = MOMENTUM_DECAY * momentum_ref[rows, :] + clip * approx
+        momentum[rows, :] = mom
+        send_out(momentum, momentum_out, rows, store_sem.at[b, 0])
+        weight[rows, :] = weight_ref[rows, :] - RATE_MATRIX * mom
+        send_out(weight, weight_out, rows, store_sem.at[b, 1])
+        matrix[rows, :] = matrix_ref[rows, :] - approx * (1.0 / count)
+        send_out(matrix, error_out.at[0], rows, store_sem.at[b, 2])
+
+    row = lax.broadcasted_iota(jnp.int32, (16, 1), 0)
+    rate = jnp.where(row < 6, RATE_GAIN, jnp.where(row < 9, RATE_BIAS, RATE_SCALE))
+    mom = MOMENTUM_DECAY * small_ref[16:32, 2 * LEN : 3 * LEN] + clip * grad
+    vector_mom_out[...] = mom
+    vector_out[...] = small_ref[16:32, LEN : 2 * LEN] - rate * mom
+    loss_out[...] = vec[6:7, 0:1]
+    norm_out[...] = norm
+    fnew_out[...] = fnew
+    live_out[...] = small_ref[16:17, 3 * LEN : 3 * LEN + 1]
+    for copy in copies:
+        copy.wait()
 
 
 def local(
@@ -721,18 +852,36 @@
     sends = (lines - 1) + lines * n_narrow + lines * (n_narrow - 1)
     anywhere = pl.BlockSpec(memory_space=pl.ANY)
     vmem = pl.BlockSpec(memory_space=pltpu.VMEM)
-    ortho, fnew, vec, live_total, matrix = pl.pallas_call(
+
+    def stay(x):
+        return pltpu.with_memory_space_constraint(x, pltpu.HBM)
+
+    in_hbm = pl.BlockSpec(memory_space=pltpu.HBM)
+    small, matrix = pl.pallas_call(
         functools.partial(step_kernel, n_wide, n_narrow),
         out_shape=(
-            jax.ShapeDtypeStruct((RANK, D), F32),
-            jax.ShapeDtypeStruct((RANK, D), F32),
-            jax.ShapeDtypeStruct((16, LEN), F32),
-            jax.ShapeDtypeStruct((1, 1), F32),
+            jax.ShapeDtypeStruct((32, D), F32),
             jax.ShapeDtypeStruct((D, D), F32),
         ),
-        in_specs=[anywhere] * 4 + [vmem] * 10,
-        out_specs=(vmem, vmem, vmem, vmem, anywhere),
+        in_specs=[in_hbm] * 19,
+        out_specs=(vmem, anywhere),
         scratch_shapes=[
+            pltpu.VMEM((ROWS_DEV, LEN), jnp.int32),
+            pltpu.VMEM((ROWS_DEV, LEN), jnp.int32),
+            pltpu.VMEM((3, ROWS_DEV), jnp.int32),
+            pltpu.VMEM((1, ROWS_DEV), jnp.int32),
+            pltpu.VMEM((RANK, D), F32),
+            pltpu.VMEM((6, LEN), F32),
+            pltpu.VMEM((6, LEN), F32),
+            pltpu.VMEM((HEADS, BUCKETS), F32),
+            pltpu.VMEM((HEADS, BUCKETS), F32),
+            pltpu.VMEM((1, 1), F32),
+            pltpu.VMEM((1, 1), F32),
+            pltpu.VMEM((2 * LEN, FLAT), BF16),
+            pltpu.VMEM((BUCKETS, FLAT), BF16),
+            pltpu.VMEM((2 * LEN, BUCKETS), BF16),
+            pltpu.VMEM((16, FLAT), F32),
+            pltpu.SemaphoreType.DMA((15,)),
             pltpu.VMEM((3, TOK, D), BF16),
             pltpu.VMEM((TOK, D), BF16),
             pltpu.VMEM((D, D), F32),
@@ -744,11 +893,13 @@
             pltpu.VMEM((32, TOK), BF16),
             pltpu.VMEM((TOK, LEN), BF16),
             pltpu.VMEM((ROWS_DEV * HEADS, LEN, LEN), F32),
+            pltpu.VMEM((2, PAIRS, LEN, 2 * LEN), F32),
+            pltpu.VMEM((2, PAIRS, 2 * LEN, LEN), BF16),
             pltpu.VMEM((D, TOK), BF16),
             pltpu.VMEM((TOK, D), F32),
-            pltpu.VMEM((TOK, 1), F32),
             pltpu.VMEM((TOK, D), BF16),
             pltpu.VMEM((TOK, D), BF16),
+            pltpu.VMEM((TOK, 1), F32),
             pltpu.VMEM((D, D), F32),
             pltpu.VMEM((D, D), BF16),
             pltpu.VMEM((D, D), BF16),
@@ -772,33 +923,32 @@
             pltpu.SemaphoreType.DMA((2, lines)),
         ],
         compiler_params=pltpu.CompilerParams(
-            collective_id=0, has_side_effects=True, vmem_limit_bytes=60 * 2**20
+            collective_id=0, has_side_effects=True, vmem_limit_bytes=(48 if blocks == 1 else 60) * 2**20
         ),
         name="step",
     )(
-        projected,
-        layer_input,
-        out_weight,
-        errors,
-        segment_ids.reshape(ROWS_DEV, LEN),
-        pad_mask.reshape(ROWS_DEV, LEN),
-        roles,
-        labelled.reshape(1, ROWS_DEV),
-        factors,
-        norm_gain.reshape(1, D),
-        position_bias.reshape(1, FLAT),
+        stay(projected),
+        stay(layer_input),
+        stay(out_weight),
+        stay(errors),
+        stay(segment_ids.reshape(ROWS_DEV, LEN)),
+        stay(pad_mask.reshape(ROWS_DEV, LEN)),
+        stay(roles.T),
+        stay(labelled.reshape(1, ROWS_DEV)),
+        stay(factors),
+        stay(norm_gain.reshape(6, LEN)),
+        stay(gain_momentum.reshape(6, LEN)),
+        stay(position_bias.T),
+        stay(bias_momentum.T),
         log_scale.reshape(1, 1),
-        jnp.asarray(diagonal_onehot(), BF16),
-        jnp.asarray(head_mask()),
-    )
-    padding = jnp.zeros((16 * LEN - D - FLAT - 1,), F32)
-    vector = jnp.concatenate([norm_gain, position_bias.reshape(-1), log_scale, padding])
-    vector_mom = jnp.concatenate([gain_momentum, bias_momentum.reshape(-1), scale_momentum, padding])
-    whole = lambda *shape: pl.BlockSpec(shape, lambda i: (0,) * len(shape))
-    rows = pl.BlockSpec((256, D), lambda i: (i, 0))
+        scale_momentum.reshape(1, 1),
+        stay(jnp.asarray(diagonal_onehot(FLAT), BF16)),
+        stay(jnp.asarray(bucket_spread(), BF16)),
+        stay(jnp.asarray(diagonal_onehot(BUCKETS), BF16)),
+        stay(jnp.asarray(head_mask())),
+    )
     outs = pl.pallas_call(
         functools.partial(update_kernel, count),
-        grid=(3,),
         out_shape=(
             jax.ShapeDtypeStruct((D, D), F32),
             jax.ShapeDtypeStruct((D, D), F32),
@@ -807,38 +957,21 @@
             jax.ShapeDtypeStruct((16, LEN), F32),
             jax.ShapeDtypeStruct((1, 1), F32),
             jax.ShapeDtypeStruct((1, 1), F32),
+            jax.ShapeDtypeStruct((RANK, D), F32),
+            jax.ShapeDtypeStruct((1, 1), F32),
         ),
-        in_specs=[
-            whole(RANK, D),
-            whole(RANK, D),
-            whole(16, LEN),
-            rows,
-            rows,
-            rows,
-            whole(16, LEN),
-            whole(16, LEN),
+        in_specs=[vmem] * 4,
+        out_specs=(anywhere,) * 3 + (vmem,) * 6,
+        scratch_shapes=[
+            pltpu.VMEM((D, D), F32),
+            pltpu.VMEM((D, D), F32),
+            pltpu.VMEM((D, D), F32),
+            pltpu.SemaphoreType.DMA((3, 3)),
         ],
-        out_specs=(
-            rows,
-            rows,
-            pl.BlockSpec((1, 256, D), lambda i: (0, i, 0)),
-            whole(16, LEN),
-            whole(16, LEN),
-            whole(1, 1),
-            whole(1, 1),
-        ),
+        compiler_params=pltpu.CompilerParams(vmem_limit_bytes=24 * 2**20),
         name="update",
-    )(
-        ortho,
-        fnew,
-        vec,
-        out_weight,
-        out_momentum,
-        matrix,
-        vector.reshape(16, LEN),
-        vector_mom.reshape(16, LEN),
-    )
-    weight_new, weight_mom, errors_new, vec_new, vec_mom, loss, norm = outs
+    )(small, matrix, out_weight, out_momentum)
+    weight_new, weight_mom, errors_new, vec_new, vec_mom, loss, norm, fnew, live_total = outs
     size = D + FLAT + 1
     return (
         weight_new,

time: 85.6 us -> 57.3 us (0.67)
  Pallas kernels: 75.2 us -> 55 us
  local copies, waits for them, and re-layouts: 6.32 us -> 0.01 us
  between operations: 3.74 us -> 2.14 us
    pallas_call x1, Pallas kernels: 67.1 us -> 50.9 us  [local(): pl.pallas_call(functools.partial(step_kernel, n_wide, n_narrow), out_shap...]
    pallas_call x1, Pallas kernels: 8.08 us -> 4.11 us  [local(): pl.pallas_call(functools.partial(update_kernel, count), out_shape=(jax.Sh...]
    unnamed x12 -> x4, local copies, waits for them, and re-layouts: 2.84 us -> 0.01 us
    reshape x4 -> x0, local copies, waits for them, and re-layouts: 2.14 us -> none  [the longest x1 1.27 us: local(): norm_gain.reshape(1, D)]
    concatenate x2 -> x0, local copies, waits for them, and re-layouts: 1.34 us -> none  [the longest x1 0.67 us: local(): jnp.concatenate([norm_gain, position_bias.reshape(-1), log_scale, padding])]
where the time goes in v2:
time: 57.3 us; the launch traced here: 57.1 us
  Pallas kernels  55 us (96%)
  between operations  2.14 us (4%)
    pallas_call x1, Pallas kernels, local(): pl.pallas_call(functools.partial(step_kernel, n_wide, n_narrow), out_shap...  50.9 us
    pallas_call x1, Pallas kernels, local(): pl.pallas_call(functools.partial(update_kernel, count), out_shape=(jax.Sh...  4.11 us

profile of v2, /device:TPU:0, one launch (start us, length us, event | category | flops | bytes accessed | tf_op | source)
XLA Modules:
  0.0 57.1 jit_solution(5818644079422704503)
XLA Ops:
  1.9 0.0 copy-start
  1.9 0.0 copy-start.1
  2.0 50.9 %step.1 = (f32[32,768]{1,0:T(8,128)S(1)}, f32[768,768]{1,0:T(8,128)S(1)}) custom-call(bf16[3,1024,768]{2,1,0:T(8,128)(2,1)} %proj_hbm.1, bf16[1024,768]{1,0:T(8,128)(2,1)} %resid_hbm.1, f32[768,768]{1,0:T(8,128)} %weight_ref.1, f32[1,768,768]{2,1,0:T(8,128)} %error_hbm.1, s32[8,128]{1,0:T(8,128)} %bitcast.21, s32[8,128]{1,0:T(8,128)} %bitcast.22, ...), custom_call_target="tpu_custom_call" | custom-call | tf_op jit(solution)/shard_map/step/pallas_call | solution.py:860
  52.8 0.0 copy-done
  52.8 0.0 copy-done.1
  52.8 4.1 %update.1 = (f32[768,768]{1,0:T(8,128)}, f32[768,768]{1,0:T(8,128)}, f32[1,768,768]{2,1,0:T(8,128)}, f32[16,128]{1,0:T(8,128)}, f32[16,128]{1,0:T(8,128)}, /*ind...) custom-call(f32[32,768]{1,0:T(8,128)S(1)} %get-tuple-element.20.small_ref, ...), custom_call_target="tpu_custom_call" | custom-call | tf_op jit(solution)/shard_map/update/pallas_call | solution.py:950
Async XLA Ops:
  1.9 50.9 %copy-start = (f32[768,768]{1,0:T(8,128)S(1)}, f32[768,768]{1,0:T(8,128)}, u32[]{:S(2)}) copy-start(f32[768,768]{1,0:T(8,128)} %weight_ref.1) | copy-start | bytes 7077892
  1.9 50.9 %copy-start.1 = (f32[768,768]{1,0:T(8,128)S(1)}, f32[768,768]{1,0:T(8,128)}, u32[]{:S(2)}) copy-start(f32[768,768]{1,0:T(8,128)} %momentum_ref.1) | copy-start | bytes 7077892

commit v3 on v2

--- a/solution.py
+++ b/solution.py
@@ -118,6 +118,7 @@
     resid_hbm,
     weight_hbm,
     error_hbm,
+    momentum_hbm,
     seg_hbm,
     pad_hbm,
     roles_hbm,
@@ -135,6 +136,8 @@
     head_mask_hbm,
     small_ref,
     matrix_hbm,
+    weight_keep,
+    momentum_keep,
     seg_ref,
     pad_ref,
     roles_ref,
@@ -162,9 +165,12 @@
     member,
     member_t,
     probs,
-    score_rows,
-    prob_rows,
+    score_even,
+    score_odd,
+    prob_even,
+    prob_odd,
     mixed_t,
+    wide_rows,
     zed,
     zed_high,
     zed_low,
@@ -194,105 +200,93 @@
     count = n_wide * n_narrow
     lines = n_wide // 2
     spots = 2 * n_narrow
-    cross = n_narrow
     wide = lax.axis_index("wide")
     narrow = lax.axis_index("narrow")
     me = wide * n_narrow + narrow
     line = wide // 2
     side = wide % 2
     spot = side * n_narrow + narrow
-    cell = side * (n_narrow // 2) + narrow // 2
-
-    def spot_device(k):
-        other = (spot + k) % spots
-        return other, (line * 2 + other // n_narrow, other % n_narrow)
+
+    y_size = n_narrow // 2
+    row_at, core = narrow // 2, narrow % 2
+    offsets = sorted(
+        (
+            (dx, dy, dc)
+            for dx in range(2)
+            for dy in range(y_size)
+            for dc in range(2)
+            if dx or dy or dc
+        ),
+        key=lambda d: (-(d[0] > 0) - (d[1] > 0), -d[2]),
+    )
+    far_lines = sorted(range(1, lines), key=lambda k: -min(k, lines - k))
+
+    def spot_device(d):
+        dx, dy, dc = d
+        other_side = (side + dx) % 2
+        other_narrow = (row_at + dy) % y_size * 2 + (core + dc) % 2
+        return other_side * n_narrow + other_narrow, (line * 2 + other_side, other_narrow)
 
     def line_device(k):
         other = (line + k) % lines
         return other, (other * 2 + side, narrow)
 
-    def cell_device(k):
-        other = (cell + k) % cross
-        return other // (n_narrow // 2), (other % (n_narrow // 2)) * 2 + narrow % 2
+    def other_line(k):
+        return k + (k - line + lines) // lines
+
+    cells = [d for d in offsets if not d[2]]
 
     sibling = (wide, narrow + 1 - 2 * (narrow % 2))
 
-    small_copies = [
-        pltpu.make_async_copy(source, target, small_sem.at[k])
+    def load(source, target, sem):
+        copy = pltpu.make_async_copy(source, target, sem)
+        copy.start()
+        return copy
+
+    def load_row(r):
+        rows = pl.ds(r * LEN, LEN)
+        load(proj_hbm.at[:, rows, :], proj.at[:, rows, :], row_sem.at[r])
+
+    mask_loads = [load(seg_hbm, seg_ref, small_sem.at[0]), load(pad_hbm, pad_ref, small_sem.at[1])]
+    load_row(0)
+    bias_loads = [
+        load(bias_hbm, bias_ref, small_sem.at[2]),
+        load(diagonal_hbm, diagonal_ref, small_sem.at[3]),
+    ]
+    load_row(1)
+    load_row(2)
+    rest_loads = [
+        load(source, target, small_sem.at[4 + k])
         for k, (source, target) in enumerate(
             (
-                (seg_hbm, seg_ref),
-                (pad_hbm, pad_ref),
                 (roles_hbm, roles_ref),
                 (label_hbm, label_ref),
                 (factor_hbm, factor_ref),
                 (gain_hbm, gain_ref),
                 (gain_mom_hbm, gain_mom_ref),
-                (bias_hbm, bias_ref),
                 (bias_mom_hbm, bias_mom_ref),
                 (scale_hbm, scale_ref),
                 (scale_mom_hbm, scale_mom_ref),
                 (onehot_hbm, onehot_ref),
                 (spread_hbm, spread_ref),
-                (diagonal_hbm, diagonal_ref),
                 (head_mask_hbm, head_mask_ref),
             )
         )
     ]
-    for copy in small_copies:
-        copy.start()
-    for r in range(ROWS_DEV):
-        rows = pl.ds(r * LEN, LEN)
-        pltpu.make_async_copy(proj_hbm.at[:, rows, :], proj.at[:, rows, :], row_sem.at[r]).start()
-    weight_copy = pltpu.make_async_copy(weight_hbm, weight, load_sem.at[0])
-    weight_copy.start()
-    resid_copy = pltpu.make_async_copy(resid_hbm, resid, resid_sem)
-    resid_copy.start()
-    error_copy = pltpu.make_async_copy(error_hbm.at[0], error, load_sem.at[1])
-    error_copy.start()
     barrier = pltpu.get_barrier_semaphore()
-    for k in range(1, spots):
-        pl.semaphore_signal(barrier, inc=1, device_id=spot_device(k)[1], device_id_type=MESH)
-    for k in range(1, lines):
+    for d in offsets:
+        pl.semaphore_signal(barrier, inc=1, device_id=spot_device(d)[1], device_id_type=MESH)
+    for k in far_lines:
         pl.semaphore_signal(barrier, inc=1, device_id=line_device(k)[1], device_id_type=MESH)
 
-    for copy in small_copies:
+    for copy in mask_loads:
         copy.wait()
-    high, middle, low = parts_of(bias_ref[...])
-    gap = jnp.zeros((4, BUCKETS), F32)
-    diag_bias = folded(
-        nt(
-            jnp.concatenate([high, gap, middle, gap, low, gap], axis=0).astype(BF16),
-            diagonal_ref[...],
-        ),
-        16,
-    )
-    row8 = lax.broadcasted_iota(jnp.int32, (8, 1), 0)
-    for h in range(HEADS):
-        sheared = jnp.broadcast_to(diag_bias[h : h + 1, :], (8, 2 * LEN))
-        for bit in (1, 2, 4):
-            sheared = jnp.where((row8 & bit) != 0, pltpu.roll(sheared, bit, 1), sheared)
-        bias_table[h, 0:8, :] = sheared[:, :LEN]
-        for a in range(1, LEN // 8):
-            bias_table[h, 8 * a : 8 * a + 8, :] = pltpu.roll(sheared, 8 * a, 1)[:, :LEN]
-
     code = jnp.where(pad_ref[...] == 1, seg_ref[...], 3).astype(F32)
     seg_f = seg_ref[...].astype(F32)
     fill = jnp.zeros((LEN - 16, LEN), F32)
     code_t = jnp.concatenate([code, seg_f, fill], axis=0).T
-    roles_f = roles_ref[...].astype(F32)
     lane = lax.broadcasted_iota(jnp.int32, (1, LEN), 1)
-    slot = lane % 32
-    row_of = lax.broadcasted_iota(jnp.int32, (32, 1), 0)
-    same = lax.broadcasted_iota(jnp.int32, (8, 8), 0) == lax.broadcasted_iota(jnp.int32, (8, 8), 1)
-
-    def column_of(row):
-        return jnp.sum(jnp.where(same, row, 0.0), axis=1, keepdims=True)
-
-    role_col = jnp.concatenate(
-        [column_of(roles_f[k : k + 1, :]) for k in range(3)] + [jnp.full((8, 1), 9.0, F32)], axis=0
-    )
-    sentence = lax.broadcasted_iota(jnp.int32, (1, LEN), 1).astype(F32)
+    sentence = lane.astype(F32)
     for r in range(ROWS_DEV):
         code_col = code_t[:, r : r + 1]
         seg_col = code_t[:, 8 + r : 9 + r]
@@ -300,32 +294,22 @@
             (sentence < 3.0) & (sentence != code_col), MASKED, 0.0
         ).astype(BF16)
         query_extra[r] = jnp.where(sentence == seg_col, 1.0, 0.0).astype(BF16)
-        role_lane = jnp.where(
-            slot < 8,
-            roles_f[0:1, r : r + 1],
-            jnp.where(slot < 16, roles_f[1:2, r : r + 1], roles_f[2:3, r : r + 1]),
-        )
-        role_lane = jnp.where((slot < 24) & (slot % 8 == r), role_lane, 9.0)
-        member_t[r * LEN : (r + 1) * LEN, :] = jnp.where(role_lane == code_col, 1.0, 0.0).astype(
-            BF16
-        )
-        member[:, r * LEN : (r + 1) * LEN] = jnp.where(
-            (role_col == code[r : r + 1, :]) & (row_of % 8 == r), 1.0, 0.0
-        ).astype(BF16)
-    counts = jnp.sum(member[...].astype(F32), axis=1, keepdims=True)[0:24]
 
     first = jnp.where(lane < HEAD_DIM, 1.0, 0.0).astype(BF16)
     second = jnp.where(lane < HEAD_DIM, 0.0, 1.0).astype(BF16)
     nothing = jnp.zeros((HEAD_DIM, LEN), BF16)
 
+    score_rows = (score_even, score_odd)
+    prob_rows = (prob_even, prob_odd)
+
     def rows_of(r):
-        return pl.ds(r * LEN if isinstance(r, int) else pl.multiple_of(r * LEN, LEN), LEN)
+        return slice(r * LEN, (r + 1) * LEN)
 
     def arrive(r):
         rows = rows_of(r)
         pltpu.make_async_copy(proj_hbm.at[:, rows, :], proj.at[:, rows, :], row_sem.at[r]).wait()
 
-    def score(r, p, k):
+    def score(r, p):
         rows = rows_of(r)
         cols = slice(p * LEN, (p + 1) * LEN)
         query = proj[0, rows, cols]
@@ -338,18 +322,18 @@
             ],
             axis=0,
         )
-        score_rows[k, p] = nt(left, right)
-
-    def soften(r, p, k):
+        score_rows[r % 2][p] = nt(left, right)
+
+    def soften(r, p):
         for half in range(2):
             head = 2 * p + half
-            part = score_rows[k, p, :, half * LEN : (half + 1) * LEN] + bias_table[head]
+            part = score_rows[r % 2][p, :, half * LEN : (half + 1) * LEN] + bias_table[head]
             part = jnp.exp(part - jnp.max(part, axis=0, keepdims=True))
             part = part * (1.0 / jnp.sum(part, axis=0, keepdims=True))
             probs[r * HEADS + head] = part
-            prob_rows[k, p, half * LEN : (half + 1) * LEN, :] = part.astype(BF16)
-
-    def mix(r, p, k):
+            prob_rows[r % 2][p, half * LEN : (half + 1) * LEN, :] = part.astype(BF16)
+
+    def mix(r, p):
         rows = rows_of(r)
         cols = slice(p * LEN, (p + 1) * LEN)
         value_t = proj[2, rows, cols].T
@@ -360,55 +344,103 @@
             ],
             axis=0,
         )
-        mixed_t[cols, rows] = nn(left, prob_rows[k, p]).astype(BF16)
+        mixed_t[cols, rows] = nn(left, prob_rows[r % 2][p]).astype(BF16)
 
     arrive(0)
     for p in range(PAIRS):
-        score(0, p, 0)
-    arrive(1)
-    for p in range(PAIRS):
-        score(1, p, 1)
-        soften(0, p, 0)
-
-    def attend(i, carry):
-        r = 2 * i + 2
-        arrive(r)
-        for p in range(PAIRS):
-            score(r, p, 0)
-            mix(r - 2, p, 0)
-            soften(r - 1, p, 1)
-        arrive(r + 1)
-        for p in range(PAIRS):
-            score(r + 1, p, 1)
-            mix(r - 1, p, 1)
-            soften(r, p, 0)
-        return carry
-
-    lax.fori_loop(0, ROWS_DEV // 2 - 1, attend, 0)
-    for p in range(PAIRS):
-        mix(ROWS_DEV - 2, p, 0)
-        soften(ROWS_DEV - 1, p, 1)
-    for p in range(PAIRS):
-        mix(ROWS_DEV - 1, p, 1)
-
-    weight_copy.wait()
-    weight_low[...] = weight[...].astype(BF16)
-    resid_copy.wait()
-    for c in range(4):
+        score(0, p)
+    for r in range(3, ROWS_DEV):
+        load_row(r)
+
+    for copy in bias_loads:
+        copy.wait()
+    high, middle, low = parts_of(bias_ref[...])
+    gap = jnp.zeros((4, BUCKETS), F32)
+    diag_bias = folded(
+        nt(
+            jnp.concatenate([high, gap, middle, gap, low, gap], axis=0).astype(BF16),
+            diagonal_ref[...],
+        ),
+        16,
+    )
+    row8 = lax.broadcasted_iota(jnp.int32, (8, 1), 0)
+    for h in range(HEADS):
+        sheared = jnp.broadcast_to(diag_bias[h : h + 1, :], (8, 2 * LEN))
+        for bit in (1, 2, 4):
+            sheared = jnp.where((row8 & bit) != 0, pltpu.roll(sheared, bit, 1), sheared)
+        bias_table[h, 0:8, :] = sheared[:, :LEN]
+        for a in range(1, LEN // 8):
+            bias_table[h, 8 * a : 8 * a + 8, :] = pltpu.roll(sheared, 8 * a, 1)[:, :LEN]
+
+    for copy in rest_loads:
+        copy.wait()
+    roles_f = roles_ref[...].astype(F32)
+    slot = lane % 32
+    row_of = lax.broadcasted_iota(jnp.int32, (32, 1), 0)
+    same = lax.broadcasted_iota(jnp.int32, (8, 8), 0) == lax.broadcasted_iota(jnp.int32, (8, 8), 1)
+
+    def column_of(row):
+        return jnp.sum(jnp.where(same, row, 0.0), axis=1, keepdims=True)
+
+    role_col = jnp.concatenate(
+        [column_of(roles_f[k : k + 1, :]) for k in range(3)] + [jnp.full((8, 1), 9.0, F32)], axis=0
+    )
+    for r in range(ROWS_DEV):
+        role_lane = jnp.where(
+            slot < 8,
+            roles_f[0:1, r : r + 1],
+            jnp.where(slot < 16, roles_f[1:2, r : r + 1], roles_f[2:3, r : r + 1]),
+        )
+        role_lane = jnp.where((slot < 24) & (slot % 8 == r), role_lane, 9.0)
+        member_t[r * LEN : (r + 1) * LEN, :] = jnp.where(
+            role_lane == code_t[:, r : r + 1], 1.0, 0.0
+        ).astype(BF16)
+        member[:, r * LEN : (r + 1) * LEN] = jnp.where(
+            (role_col == code[r : r + 1, :]) & (row_of % 8 == r), 1.0, 0.0
+        ).astype(BF16)
+
+    def project(c):
         rows = slice(c * 256, (c + 1) * 256)
         zed[rows, :] = resid[rows, :].astype(F32) + tn(mixed_t[:, rows], weight_low[...])
 
-    for b in range(TOK // 32):
-        rows = slice(b * 32, (b + 1) * 32)
-        hidden = zed[rows, :]
-        inv = lax.rsqrt(jnp.sum(hidden * hidden, axis=1, keepdims=True) * (1.0 / D) + EPSILON)
-        hidden = hidden * inv
-        zed[rows, :] = hidden
-        rms_inv[rows, :] = inv
-        high = hidden.astype(BF16)
-        zed_high[rows, :] = high
-        zed_low[rows, :] = (hidden - high.astype(F32)).astype(BF16)
-    sums = nn(member[...], zed_high[...]) + nn(member[...], zed_low[...])
+    def normalise():
+        for b in range(TOK // 32):
+            rows = slice(b * 32, (b + 1) * 32)
+            hidden = zed[rows, :]
+            inv = lax.rsqrt(jnp.sum(hidden * hidden, axis=1, keepdims=True) * (1.0 / D) + EPSILON)
+            hidden = hidden * inv
+            zed[rows, :] = hidden
+            rms_inv[rows, :] = inv
+            high = hidden.astype(BF16)
+            zed_high[rows, :] = high
+            zed_low[rows, :] = (hidden - high.astype(F32)).astype(BF16)
+        return nn(member[...], zed_high[...]) + nn(member[...], zed_low[...])
+
+    for step in range(1, ROWS_DEV + 2):
+        if step < ROWS_DEV:
+            arrive(step)
+        for p in range(PAIRS):
+            if step < ROWS_DEV:
+                score(step, p)
+            if step > 1:
+                mix(step - 2, p)
+            if step <= ROWS_DEV:
+                soften(step - 1, p)
+        if step == 2:
+            weight_copy = load(weight_hbm, weight, load_sem.at[0])
+            resid_copy = load(resid_hbm, resid, resid_sem)
+    weight_copy.wait()
+    resid_copy.wait()
+    weight_low[...] = weight[...].astype(BF16)
+    for c in range(4):
+        project(c)
+    sums = normalise()
+    error_copy = load(error_hbm.at[0], error, load_sem.at[1])
+    keep_copies = [
+        load(momentum_hbm, momentum_keep, load_sem.at[2]),
+        load(weight, weight_keep, load_sem.at[3]),
+    ]
+    counts = jnp.sum(member[...].astype(F32), axis=1, keepdims=True)[0:24]
     gain_rows = gain_ref[...]
     gain = jnp.concatenate([gain_rows[k : k + 1, :] for k in range(6)], axis=1)
     zed_mean = sums[0:24] / counts
@@ -453,23 +485,16 @@
             device_id_type=MESH,
         ).wait_recv()
 
-    for k in range(1, lines):
+    line_order = [line] + [other_line(k) for k in range(lines - 1)]
+    for k in far_lines:
         send_block(me, line_device(k)[1])
     for k in range(lines):
-        block_line, (block_wide, _) = line_device(k)
-        block = block_wide * n_narrow + narrow
+        block = (line_order[k] * 2 + side) * n_narrow + narrow
         if k:
             await_block(block)
-        for j in range(1, cross):
-            other_side, other_narrow = cell_device(j)
-            send_block(block, (line * 2 + other_side, other_narrow))
+        for d in cells:
+            send_block(block, spot_device(d)[1])
         send_block(block, sibling)
-    for k in range(lines):
-        for j in range(1, cross):
-            other_side, other_narrow = cell_device(j)
-            block = ((line + k) % lines * 2 + other_side) * n_narrow + other_narrow
-            await_block(block)
-            send_block(block, sibling)
 
     error_copy.wait()
     factor_parts = stacked_parts(factor_ref[...])
@@ -501,10 +526,16 @@
     small_ref[16:32, 2 * LEN : 3 * LEN] = packed(gain_mom_ref[...], flat_bias(bias_mom_ref[...]), scale_mom_ref[...])
 
     for k in range(lines):
-        for j in range(cross):
-            other_side, other_narrow = cell_device(j)
+        for d in cells[::-1]:
+            _, (other_wide, other_narrow) = spot_device(d)
+            block = (line_order[k] * 2 + other_wide % 2) * n_narrow + other_narrow
+            await_block(block)
+            send_block(block, sibling)
+    for k in range(lines):
+        for d in [(0, 0, 0)] + cells[::-1]:
+            _, (other_wide, other_narrow) = spot_device(d)
             block = (
-                ((line + k) % lines * 2 + other_side) * n_narrow
+                (line_order[k] * 2 + other_wide % 2) * n_narrow
                 + other_narrow
                 + 1
                 - 2 * (narrow % 2)
@@ -604,9 +635,10 @@
     shares = jnp.concatenate(
         [high, wide_gap, middle, wide_gap, low, wide_gap, jnp.zeros((32, D), F32)], axis=0
     ).astype(BF16)
-    for c in range(4):
-        rows = slice(c * 256, (c + 1) * 256)
-        zed_grad = nn(member_t[rows, :], shares)
+    wide_rows[...] = nn(member_t[...], shares)
+    for b in range(TOK // 32):
+        rows = slice(b * 32, (b + 1) * 32)
+        zed_grad = wide_rows[rows, :]
         zed_rows = zed[rows, :]
         level = jnp.sum(zed_grad * zed_rows, axis=1, keepdims=True) * (1.0 / D)
         branch[rows, :] = (rms_inv[rows, :] * (zed_grad - zed_rows * level)).astype(BF16)
@@ -637,27 +669,29 @@
 
     def start_sum(which, plane):
         return [
-            send_to(plane, spot, spot_device(k)[1], plane_send.at[which, k], plane_recv.at[which])
-            for k in range(1, spots)
+            send_to(plane, spot, spot_device(d)[1], plane_send.at[which, k], plane_recv.at[which])
+            for k, d in enumerate(offsets)
         ]
 
-    def finish_sum(which, plane, started, along):
-        for k in range(1, spots):
-            await_from(plane, spot_device(k)[0], plane_send.at[which, 0], plane_recv.at[which])
+    def middle_sum(which, plane, along):
+        for d in offsets[::-1]:
+            await_from(plane, spot_device(d)[0], plane_send.at[which, 0], plane_recv.at[which])
         total = plane[0]
         for k in range(1, spots):
             total = total + plane[k]
         along[line] = total
-        second = [
+        return [
             send_to(along, line, line_device(k)[1], line_send.at[which, k], line_recv.at[which])
-            for k in range(1, lines)
+            for k in far_lines
         ]
-        for k in range(1, lines):
+
+    def finish_sum(which, along, started):
+        for k in far_lines[::-1]:
             await_from(along, line_device(k)[0], line_send.at[which, 0], line_recv.at[which])
         total = along[0]
         for k in range(1, lines):
             total = total + along[k]
-        for copy in started + second:
+        for copy in started:
             copy.wait_send()
         return total
 
@@ -684,6 +718,7 @@
     for c in range(4):
         rows = slice(c * 256, (c + 1) * 256)
         mixed_grad[rows, :] = nt(branch[rows, :], weight_low[...]).astype(BF16)
+    started = started + middle_sum(0, plane1, line1)
     for p in range(PAIRS):
         cols = slice(p * LEN, (p + 1) * LEN)
 
@@ -719,7 +754,7 @@
     )
     bias_grad = jnp.sum(by_bucket * head_mask_ref[...], axis=0, keepdims=True)
 
-    total = finish_sum(0, plane1, started, line1)
+    total = finish_sum(0, line1, started)
     small_ref[16:24, 0:LEN] = total[:, D:WIDTH]
     ortho = total[:, 0:D]
     rank_row = lax.broadcasted_iota(jnp.int32, (RANK, 1), 0)
@@ -741,12 +776,15 @@
         axis=0,
     )
     started = start_sum(1, plane2)
-    total = finish_sum(1, plane2, started, line2)
+    started = started + middle_sum(1, plane2, line2)
+    total = finish_sum(1, line2, started)
     small_ref[8:16, :] = total[:, 0:D]
     small_ref[24:32, 0:LEN] = total[:, D:WIDTH]
     small_ref[16:32, 3 * LEN : 4 * LEN] = jnp.broadcast_to(live_total, (16, LEN))
     small_ref[16:32, 4 * LEN : D] = jnp.zeros((16, D - 4 * LEN), F32)
     matrix_copy.wait()
+    for copy in keep_copies:
+        copy.wait()
 
 
 def update_kernel(
@@ -771,6 +809,25 @@
 ):
     ortho = small_ref[0:8, :]
     fnew = small_ref[8:16, :]
+    oh, om, ol = parts_of(ortho)
+    fh, fm, fl = parts_of(fnew)
+    pad = jnp.zeros((16, D), F32)
+    left = jnp.concatenate([oh, oh, om, om, oh, ol, pad], axis=0).astype(BF16)
+    right = jnp.concatenate([fh, fm, fh, fm, fl, fh, pad], axis=0).astype(BF16)
+    copies = []
+
+    def send_out(source, target, rows, sem):
+        copy = pltpu.make_async_copy(source.at[rows, :], target.at[rows, :], sem)
+        copy.start()
+        copies.append(copy)
+
+    for b in range(3):
+        rows = slice(b * 256, (b + 1) * 256)
+        approx = tn(left[:, rows], right)
+        weight[rows, :] = approx
+        matrix[rows, :] = matrix_ref[rows, :] - approx * (1.0 / count)
+        send_out(matrix, error_out.at[0], rows, store_sem.at[b, 2])
+
     square = jnp.zeros((RANK, 1), F32)
     for k in range(RANK):
         left = jnp.sum(ortho * ortho[k : k + 1, :], axis=1, keepdims=True)
@@ -789,28 +846,13 @@
     norm = jnp.sqrt(square)
     clip = CLIP_NORM / jnp.maximum(norm, CLIP_NORM)
 
-    oh, om, ol = parts_of(ortho)
-    fh, fm, fl = parts_of(fnew)
-    pad = jnp.zeros((16, D), F32)
-    left = jnp.concatenate([oh, oh, om, om, oh, ol, pad], axis=0).astype(BF16)
-    right = jnp.concatenate([fh, fm, fh, fm, fl, fh, pad], axis=0).astype(BF16)
-    copies = []
-
-    def send_out(source, target, rows, sem):
-        copy = pltpu.make_async_copy(source.at[rows, :], target.at[rows, :], sem)
-        copy.start()
-        copies.append(copy)
-
     for b in range(3):
         rows = slice(b * 256, (b + 1) * 256)
-        approx = tn(left[:, rows], right)
-        mom = MOMENTUM_DECAY * momentum_ref[rows, :] + clip * approx
+        mom = MOMENTUM_DECAY * momentum_ref[rows, :] + clip * weight[rows, :]
         momentum[rows, :] = mom
         send_out(momentum, momentum_out, rows, store_sem.at[b, 0])
         weight[rows, :] = weight_ref[rows, :] - RATE_MATRIX * mom
         send_out(weight, weight_out, rows, store_sem.at[b, 1])
-        matrix[rows, :] = matrix_ref[rows, :] - approx * (1.0 / count)
-        send_out(matrix, error_out.at[0], rows, store_sem.at[b, 2])
 
     row = lax.broadcasted_iota(jnp.int32, (16, 1), 0)
     rate = jnp.where(row < 6, RATE_GAIN, jnp.where(row < 9, RATE_BIAS, RATE_SCALE))
@@ -857,14 +899,16 @@
         return pltpu.with_memory_space_constraint(x, pltpu.HBM)
 
     in_hbm = pl.BlockSpec(memory_space=pltpu.HBM)
-    small, matrix = pl.pallas_call(
+    kept = pl.pallas_call(
         functools.partial(step_kernel, n_wide, n_narrow),
         out_shape=(
             jax.ShapeDtypeStruct((32, D), F32),
             jax.ShapeDtypeStruct((D, D), F32),
+            jax.ShapeDtypeStruct((D, D), F32),
+            jax.ShapeDtypeStruct((D, D), F32),
         ),
-        in_specs=[in_hbm] * 19,
-        out_specs=(vmem, anywhere),
+        in_specs=[in_hbm] * 20,
+        out_specs=(vmem, anywhere, anywhere, anywhere),
         scratch_shapes=[
             pltpu.VMEM((ROWS_DEV, LEN), jnp.int32),
             pltpu.VMEM((ROWS_DEV, LEN), jnp.int32),
@@ -893,9 +937,12 @@
             pltpu.VMEM((32, TOK), BF16),
             pltpu.VMEM((TOK, LEN), BF16),
             pltpu.VMEM((ROWS_DEV * HEADS, LEN, LEN), F32),
-            pltpu.VMEM((2, PAIRS, LEN, 2 * LEN), F32),
-            pltpu.VMEM((2, PAIRS, 2 * LEN, LEN), BF16),
+            pltpu.VMEM((PAIRS, LEN, 2 * LEN), F32),
+            pltpu.VMEM((PAIRS, LEN, 2 * LEN), F32),
+            pltpu.VMEM((PAIRS, 2 * LEN, LEN), BF16),
+            pltpu.VMEM((PAIRS, 2 * LEN, LEN), BF16),
             pltpu.VMEM((D, TOK), BF16),
+            pltpu.VMEM((TOK, D), F32),
             pltpu.VMEM((TOK, D), F32),
             pltpu.VMEM((TOK, D), BF16),
             pltpu.VMEM((TOK, D), BF16),
@@ -913,7 +960,7 @@
             pltpu.VMEM((lines, RANK, WIDTH), F32),
             pltpu.SemaphoreType.DMA((ROWS_DEV,)),
             pltpu.SemaphoreType.DMA,
-            pltpu.SemaphoreType.DMA((2,)),
+            pltpu.SemaphoreType.DMA((4,)),
             pltpu.SemaphoreType.DMA,
             pltpu.SemaphoreType.DMA((sends,)),
             pltpu.SemaphoreType.DMA((count,)),
@@ -923,7 +970,7 @@
             pltpu.SemaphoreType.DMA((2, lines)),
         ],
         compiler_params=pltpu.CompilerParams(
-            collective_id=0, has_side_effects=True, vmem_limit_bytes=(48 if blocks == 1 else 60) * 2**20
+            collective_id=0, has_side_effects=True, vmem_limit_bytes=(45 if blocks == 1 else 60) * 2**20
         ),
         name="step",
     )(
@@ -931,6 +978,7 @@
         stay(layer_input),
         stay(out_weight),
         stay(errors),
+        stay(out_momentum),
         stay(segment_ids.reshape(ROWS_DEV, LEN)),
         stay(pad_mask.reshape(ROWS_DEV, LEN)),
         stay(roles.T),
@@ -970,7 +1018,7 @@
         ],
         compiler_params=pltpu.CompilerParams(vmem_limit_bytes=24 * 2**20),
         name="update",
-    )(small, matrix, out_weight, out_momentum)
+    )(*kept)
     weight_new, weight_mom, errors_new, vec_new, vec_mom, loss, norm, fnew, live_total = outs
     size = D + FLAT + 1
     return (

time: 57.3 us -> 54 us (0.942)
  Pallas kernels: 55 us -> 51.7 us
    pallas_call x1, Pallas kernels: 50.9 us -> 47.6 us  [local(): pl.pallas_call(functools.partial(step_kernel, n_wide, n_narrow), out_shap...]
where the time goes in v3:
time: 54 us; the launch traced here: 53.8 us
  Pallas kernels  51.7 us (96%)
  between operations  2.11 us (4%)
    pallas_call x1, Pallas kernels, local(): pl.pallas_call(functools.partial(step_kernel, n_wide, n_narrow), out_shap...  47.6 us
    pallas_call x1, Pallas kernels, local(): pl.pallas_call(functools.partial(update_kernel, count), out_shape=(jax.Sh...  4.14 us

profile of v3, /device:TPU:0, one launch (start us, length us, event | category | flops | bytes accessed | tf_op | source)
XLA Modules:
  0.0 53.8 jit_solution(9643397695160658507)
XLA Ops:
  1.9 47.6 %step.1 = (f32[32,768]{1,0:T(8,128)S(1)}, f32[768,768]{1,0:T(8,128)S(1)}, f32[768,768]{1,0:T(8,128)S(1)}, f32[768,768]{1,0:T(8,128)S(1)}) custom-call(bf16[3,1024,768]{2,1,0:T(8,128)(2,1)} %proj_hbm.1, bf16[1024,768]{1,0:T(8,128)(2,1)} %resid_hbm.1, f32[768,768]{1,0:T(8,128)} %weight_hbm.1, f32[1,768,768]{2,1,0:T(8,128)} %error_hbm.1, ...), custom_call_target="tpu_custom_call" | custom-call | tf_op jit(solution)/shard_map/step/pallas_call | solution.py:902
  49.5 4.1 %update.1 = (f32[768,768]{1,0:T(8,128)}, f32[768,768]{1,0:T(8,128)}, f32[1,768,768]{2,1,0:T(8,128)}, f32[16,128]{1,0:T(8,128)}, f32[16,128]{1,0:T(8,128)}, /*ind...) custom-call(f32[32,768]{1,0:T(8,128)S(1)} %get-tuple-element.22.small_ref, ...), custom_call_target="tpu_custom_call" | custom-call | tf_op jit(solution)/shard_map/update/pallas_call | solution.py:998

commit v4 on v3

--- a/solution.py
+++ b/solution.py
@@ -175,6 +175,7 @@
     zed_high,
     zed_low,
     rms_inv,
+    levels,
     matrix,
     matrix_high,
     matrix_low,
@@ -253,8 +254,8 @@
         load(bias_hbm, bias_ref, small_sem.at[2]),
         load(diagonal_hbm, diagonal_ref, small_sem.at[3]),
     ]
-    load_row(1)
-    load_row(2)
+    for r in range(1, ROWS_DEV):
+        load_row(r)
     rest_loads = [
         load(source, target, small_sem.at[4 + k])
         for k, (source, target) in enumerate(
@@ -349,8 +350,6 @@
     arrive(0)
     for p in range(PAIRS):
         score(0, p)
-    for r in range(3, ROWS_DEV):
-        load_row(r)
 
     for copy in bias_loads:
         copy.wait()
@@ -416,9 +415,11 @@
             zed_low[rows, :] = (hidden - high.astype(F32)).astype(BF16)
         return nn(member[...], zed_high[...]) + nn(member[...], zed_low[...])
 
+    for r in range(1, ROWS_DEV):
+        arrive(r)
+    weight_copy = load(weight_hbm, weight, load_sem.at[0])
+    resid_copy = load(resid_hbm, resid, resid_sem)
     for step in range(1, ROWS_DEV + 2):
-        if step < ROWS_DEV:
-            arrive(step)
         for p in range(PAIRS):
             if step < ROWS_DEV:
                 score(step, p)
@@ -426,9 +427,6 @@
                 mix(step - 2, p)
             if step <= ROWS_DEV:
                 soften(step - 1, p)
-        if step == 2:
-            weight_copy = load(weight_hbm, weight, load_sem.at[0])
-            resid_copy = load(resid_hbm, resid, resid_sem)
     weight_copy.wait()
     resid_copy.wait()
     weight_low[...] = weight[...].astype(BF16)
@@ -541,9 +539,6 @@
                 - 2 * (narrow % 2)
             )
             await_block(block)
-    for copy in sends:
-        copy.wait_send()
-
     blocks = count // GROUP
     temper = jnp.exp(scale_ref[...])
 
@@ -626,7 +621,7 @@
     loss_own = jnp.sum(live16 * (log_total - positive), axis=0, keepdims=True)
     scale_grad = jnp.sum(scale_grad, axis=0, keepdims=True)
 
-    branch, mixed_grad = zed_high, zed_low
+    branch, mixed_grad = resid, zed_low
     unit_grad = jnp.concatenate([anchor_grad[0:8], cand_grad], axis=0)
     mean_grad = inverse * (unit_grad - unit * jnp.sum(unit * unit_grad, axis=1, keepdims=True))
     gain_grad = jnp.sum(mean_grad * zed_mean, axis=0, keepdims=True)
@@ -685,14 +680,12 @@
             for k in far_lines
         ]
 
-    def finish_sum(which, along, started):
+    def finish_sum(which, along):
         for k in far_lines[::-1]:
             await_from(along, line_device(k)[0], line_send.at[which, 0], line_recv.at[which])
         total = along[0]
         for k in range(1, lines):
             total = total + along[k]
-        for copy in started:
-            copy.wait_send()
         return total
 
     scalars = jnp.where(lane == 0, loss_own, jnp.where(lane == 1, scale_grad, 0.0))
@@ -703,7 +696,7 @@
     )
     plane1[spot, :, 0:D] = row_part
     plane1[spot, :, D:WIDTH] = extra
-    started = start_sum(0, plane1)
+    sends.extend(start_sum(0, plane1))
 
     for b in range(3):
         rows = slice(b * 256, (b + 1) * 256)
@@ -718,7 +711,7 @@
     for c in range(4):
         rows = slice(c * 256, (c + 1) * 256)
         mixed_grad[rows, :] = nt(branch[rows, :], weight_low[...]).astype(BF16)
-    started = started + middle_sum(0, plane1, line1)
+    sends.extend(middle_sum(0, plane1, line1))
     for p in range(PAIRS):
         cols = slice(p * LEN, (p + 1) * LEN)
 
@@ -754,7 +747,7 @@
     )
     bias_grad = jnp.sum(by_bucket * head_mask_ref[...], axis=0, keepdims=True)
 
-    total = finish_sum(0, line1, started)
+    total = finish_sum(0, line1)
     small_ref[16:24, 0:LEN] = total[:, D:WIDTH]
     ortho = total[:, 0:D]
     rank_row = lax.broadcasted_iota(jnp.int32, (RANK, 1), 0)
@@ -775,16 +768,20 @@
         [bias_grad[:, k * LEN : (k + 1) * LEN] for k in range(3)] + [jnp.zeros((5, LEN), F32)],
         axis=0,
     )
-    started = start_sum(1, plane2)
-    started = started + middle_sum(1, plane2, line2)
-    total = finish_sum(1, line2, started)
+    sends.extend(start_sum(1, plane2))
+    for copy in sends:
+        copy.wait_send()
+    matrix_copy.wait()
+    for copy in keep_copies:
+        copy.wait()
+    last_sends = middle_sum(1, plane2, line2)
+    total = finish_sum(1, line2)
     small_ref[8:16, :] = total[:, 0:D]
     small_ref[24:32, 0:LEN] = total[:, D:WIDTH]
     small_ref[16:32, 3 * LEN : 4 * LEN] = jnp.broadcast_to(live_total, (16, LEN))
     small_ref[16:32, 4 * LEN : D] = jnp.zeros((16, D - 4 * LEN), F32)
-    matrix_copy.wait()
-    for copy in keep_copies:
-        copy.wait()
+    for copy in last_sends:
+        copy.wait_send()
 
 
 def update_kernel(
@@ -821,8 +818,8 @@
         copy.start()
         copies.append(copy)
 
-    for b in range(3):
-        rows = slice(b * 256, (b + 1) * 256)
+    for b in range(6):
+        rows = slice(b * LEN, (b + 1) * LEN)
         approx = tn(left[:, rows], right)
         weight[rows, :] = approx
         matrix[rows, :] = matrix_ref[rows, :] - approx * (1.0 / count)
@@ -846,8 +843,8 @@
     norm = jnp.sqrt(square)
     clip = CLIP_NORM / jnp.maximum(norm, CLIP_NORM)
 
-    for b in range(3):
-        rows = slice(b * 256, (b + 1) * 256)
+    for b in range(6):
+        rows = slice(b * LEN, (b + 1) * LEN)
         mom = MOMENTUM_DECAY * momentum_ref[rows, :] + clip * weight[rows, :]
         momentum[rows, :] = mom
         send_out(momentum, momentum_out, rows, store_sem.at[b, 0])
@@ -947,6 +944,7 @@
             pltpu.VMEM((TOK, D), BF16),
             pltpu.VMEM((TOK, D), BF16),
             pltpu.VMEM((TOK, 1), F32),
+            pltpu.VMEM((TOK, 1), F32),
             pltpu.VMEM((D, D), F32),
             pltpu.VMEM((D, D), BF16),
             pltpu.VMEM((D, D), BF16),
@@ -1014,7 +1012,7 @@
             pltpu.VMEM((D, D), F32),
             pltpu.VMEM((D, D), F32),
             pltpu.VMEM((D, D), F32),
-            pltpu.SemaphoreType.DMA((3, 3)),
+            pltpu.SemaphoreType.DMA((6, 3)),
         ],
         compiler_params=pltpu.CompilerParams(vmem_limit_bytes=24 * 2**20),
         name="update",

time: 54 us -> 51.5 us (0.954)
  Pallas kernels: 51.7 us -> 49.2 us
    pallas_call x1, Pallas kernels: 47.6 us -> 45.1 us  [local(): pl.pallas_call(functools.partial(step_kernel, n_wide, n_narrow), out_shap...]
where the time goes in v4:
time: 51.5 us; the launch traced here: 51.3 us
  Pallas kernels  49.2 us (96%)
  between operations  2.11 us (4%)
    pallas_call x1, Pallas kernels, local(): pl.pallas_call(functools.partial(step_kernel, n_wide, n_narrow), out_shap...  45.1 us
    pallas_call x1, Pallas kernels, local(): pl.pallas_call(functools.partial(update_kernel, count), out_shape=(jax.Sh...  4.09 us

profile of v4, /device:TPU:0, one launch (start us, length us, event | category | flops | bytes accessed | tf_op | source)
XLA Modules:
  0.0 51.3 jit_solution(14983093006914245858)
XLA Ops:
  1.9 45.1 %step.1 = (f32[32,768]{1,0:T(8,128)S(1)}, f32[768,768]{1,0:T(8,128)S(1)}, f32[768,768]{1,0:T(8,128)S(1)}, f32[768,768]{1,0:T(8,128)S(1)}) custom-call(bf16[3,1024,768]{2,1,0:T(8,128)(2,1)} %proj_hbm.1, bf16[1024,768]{1,0:T(8,128)(2,1)} %resid_hbm.1, f32[768,768]{1,0:T(8,128)} %weight_hbm.1, f32[1,768,768]{2,1,0:T(8,128)} %error_hbm.1, ...), custom_call_target="tpu_custom_call" | custom-call | tf_op jit(solution)/shard_map/step/pallas_call | solution.py:899
  47.1 4.1 %update.1 = (f32[768,768]{1,0:T(8,128)}, f32[768,768]{1,0:T(8,128)}, f32[1,768,768]{2,1,0:T(8,128)}, f32[16,128]{1,0:T(8,128)}, f32[16,128]{1,0:T(8,128)}, /*ind...) custom-call(f32[32,768]{1,0:T(8,128)S(1)} %get-tuple-element.22.small_ref, ...), custom_call_target="tpu_custom_call" | custom-call | tf_op jit(solution)/shard_map/update/pallas_call | solution.py:996

commit v5 on v4

--- a/solution.py
+++ b/solution.py
@@ -179,6 +179,7 @@
     matrix,
     matrix_high,
     matrix_low,
+    matrix_rest,
     gather,
     anchors_all,
     own_scores,
@@ -244,18 +245,16 @@
         copy.start()
         return copy
 
-    def load_row(r):
-        rows = pl.ds(r * LEN, LEN)
-        load(proj_hbm.at[:, rows, :], proj.at[:, rows, :], row_sem.at[r])
-
     mask_loads = [load(seg_hbm, seg_ref, small_sem.at[0]), load(pad_hbm, pad_ref, small_sem.at[1])]
-    load_row(0)
+    first_row = load(
+        proj_hbm.at[:, pl.ds(0, LEN), :], proj.at[:, pl.ds(0, LEN), :], row_sem.at[0]
+    )
     bias_loads = [
         load(bias_hbm, bias_ref, small_sem.at[2]),
         load(diagonal_hbm, diagonal_ref, small_sem.at[3]),
     ]
-    for r in range(1, ROWS_DEV):
-        load_row(r)
+    later = pl.ds(LEN, TOK - LEN)
+    later_rows = load(proj_hbm.at[:, later, :], proj.at[:, later, :], row_sem.at[1])
     rest_loads = [
         load(source, target, small_sem.at[4 + k])
         for k, (source, target) in enumerate(
@@ -306,10 +305,6 @@
     def rows_of(r):
         return slice(r * LEN, (r + 1) * LEN)
 
-    def arrive(r):
-        rows = rows_of(r)
-        pltpu.make_async_copy(proj_hbm.at[:, rows, :], proj.at[:, rows, :], row_sem.at[r]).wait()
-
     def score(r, p):
         rows = rows_of(r)
         cols = slice(p * LEN, (p + 1) * LEN)
@@ -347,7 +342,7 @@
         )
         mixed_t[cols, rows] = nn(left, prob_rows[r % 2][p]).astype(BF16)
 
-    arrive(0)
+    first_row.wait()
     for p in range(PAIRS):
         score(0, p)
 
@@ -415,8 +410,7 @@
             zed_low[rows, :] = (hidden - high.astype(F32)).astype(BF16)
         return nn(member[...], zed_high[...]) + nn(member[...], zed_low[...])
 
-    for r in range(1, ROWS_DEV):
-        arrive(r)
+    later_rows.wait()
     weight_copy = load(weight_hbm, weight, load_sem.at[0])
     resid_copy = load(resid_hbm, resid, resid_sem)
     for step in range(1, ROWS_DEV + 2):
@@ -465,19 +459,19 @@
         copy = pltpu.make_async_remote_copy(
             src_ref=gather.at[block],
             dst_ref=gather.at[block],
-            send_sem=gather_send.at[len(sends)],
+            send_sem=gather_send,
             recv_sem=gather_recv.at[block],
             device_id=device,
             device_id_type=MESH,
         )
         copy.start()
-        sends.append(copy)
+        sends.append(block)
 
     def await_block(block):
         pltpu.make_async_remote_copy(
             src_ref=gather.at[block],
             dst_ref=gather.at[block],
-            send_sem=gather_send.at[0],
+            send_sem=gather_send,
             recv_sem=gather_recv.at[block],
             device_id=sibling,
             device_id_type=MESH,
@@ -640,49 +634,36 @@
     by_token = folded(nt(factor_parts, branch[...]), RANK)
     row_part = row_part + folded(nt(stacked_parts(by_token), mixed_t[...]), RANK)
 
-    def send_to(buffers, mine, device, send_sem, recv_sem):
-        copy = pltpu.make_async_remote_copy(
-            src_ref=buffers.at[mine],
-            dst_ref=buffers.at[mine],
-            send_sem=send_sem,
-            recv_sem=recv_sem.at[mine],
-            device_id=device,
-            device_id_type=MESH,
-        )
-        copy.start()
-        return copy
-
-    def await_from(buffers, other, send_sem, recv_sem):
-        pltpu.make_async_remote_copy(
-            src_ref=buffers.at[other],
-            dst_ref=buffers.at[other],
-            send_sem=send_sem,
-            recv_sem=recv_sem.at[other],
-            device_id=sibling,
-            device_id_type=MESH,
-        ).wait_recv()
+    def exchange(buffers, mine, devices, send_sem, recv_sem):
+        for device in devices:
+            pltpu.make_async_remote_copy(
+                src_ref=buffers.at[mine],
+                dst_ref=buffers.at[mine],
+                send_sem=send_sem,
+                recv_sem=recv_sem,
+                device_id=device,
+                device_id_type=MESH,
+            ).start()
+
+    def bytes_of(buffers, blocks, sem):
+        part = buffers.at[pl.ds(0, blocks)]
+        return pltpu.make_async_copy(part, part, sem)
 
     def start_sum(which, plane):
-        return [
-            send_to(plane, spot, spot_device(d)[1], plane_send.at[which, k], plane_recv.at[which])
-            for k, d in enumerate(offsets)
-        ]
+        devices = [spot_device(d)[1] for d in offsets]
+        exchange(plane, spot, devices, plane_send.at[which], plane_recv.at[which])
 
     def middle_sum(which, plane, along):
-        for d in offsets[::-1]:
-            await_from(plane, spot_device(d)[0], plane_send.at[which, 0], plane_recv.at[which])
+        bytes_of(plane, spots - 1, plane_recv.at[which]).wait()
         total = plane[0]
         for k in range(1, spots):
             total = total + plane[k]
         along[line] = total
-        return [
-            send_to(along, line, line_device(k)[1], line_send.at[which, k], line_recv.at[which])
-            for k in far_lines
-        ]
+        devices = [line_device(k)[1] for k in far_lines]
+        exchange(along, line, devices, line_send.at[which], line_recv.at[which])
 
     def finish_sum(which, along):
-        for k in far_lines[::-1]:
-            await_from(along, line_device(k)[0], line_send.at[which, 0], line_recv.at[which])
+        bytes_of(along, lines - 1, line_recv.at[which]).wait()
         total = along[0]
         for k in range(1, lines):
             total = total + along[k]
@@ -696,7 +677,7 @@
     )
     plane1[spot, :, 0:D] = row_part
     plane1[spot, :, D:WIDTH] = extra
-    sends.extend(start_sum(0, plane1))
+    start_sum(0, plane1)
 
     for b in range(3):
         rows = slice(b * 256, (b + 1) * 256)
@@ -704,14 +685,17 @@
         matrix[rows, :] = full
         high = full.astype(BF16)
         matrix_high[rows, :] = high
-        matrix_low[rows, :] = (full - high.astype(F32)).astype(BF16)
+        rest = full - high.astype(F32)
+        low = rest.astype(BF16)
+        matrix_low[rows, :] = low
+        matrix_rest[rows, :] = (rest - low.astype(F32)).astype(BF16)
     matrix_copy = pltpu.make_async_copy(matrix, matrix_hbm, out_sem)
     matrix_copy.start()
 
     for c in range(4):
         rows = slice(c * 256, (c + 1) * 256)
         mixed_grad[rows, :] = nt(branch[rows, :], weight_low[...]).astype(BF16)
-    sends.extend(middle_sum(0, plane1, line1))
+    middle_sum(0, plane1, line1)
     for p in range(PAIRS):
         cols = slice(p * LEN, (p + 1) * LEN)
 
@@ -750,38 +734,47 @@
     total = finish_sum(0, line1)
     small_ref[16:24, 0:LEN] = total[:, D:WIDTH]
     ortho = total[:, 0:D]
+    row_parts = stacked_parts(ortho)
+    product = folded(
+        nn(row_parts, matrix_high[...])
+        + nn(row_parts, matrix_low[...])
+        + nn(row_parts, matrix_rest[...]),
+        RANK,
+    )
     rank_row = lax.broadcasted_iota(jnp.int32, (RANK, 1), 0)
+    weights = []
     for k in range(RANK):
         vector = ortho[k : k + 1, :]
         dots = jnp.sum(ortho * vector, axis=1, keepdims=True)
         norm = lax.rsqrt(dots[k : k + 1, :] + EPSILON)
         vector = vector * norm
-        ortho = jnp.where(
-            rank_row > k, ortho - (dots * norm) * vector, jnp.where(rank_row == k, vector, ortho)
-        )
+        weight_k = jnp.where(rank_row > k, dots * norm, 0.0)
+        ortho = jnp.where(rank_row == k, vector, ortho - weight_k * vector)
+        weights.append((norm, weight_k))
+    for k, (norm, weight_k) in enumerate(weights):
+        vector = product[k : k + 1, :] * norm
+        product = jnp.where(rank_row == k, vector, product - weight_k * vector)
     small_ref[0:8, :] = ortho
-    ortho_parts = stacked_parts(ortho)
-    plane2[spot, :, 0:D] = folded(
-        nn(ortho_parts, matrix_high[...]) + nn(ortho_parts, matrix_low[...]), RANK
-    )
+    plane2[spot, :, 0:D] = product
     plane2[spot, :, D:WIDTH] = jnp.concatenate(
         [bias_grad[:, k * LEN : (k + 1) * LEN] for k in range(3)] + [jnp.zeros((5, LEN), F32)],
         axis=0,
     )
-    sends.extend(start_sum(1, plane2))
-    for copy in sends:
-        copy.wait_send()
+    start_sum(1, plane2)
+    bytes_of(gather, len(sends), gather_send).wait()
+    bytes_of(plane1, spots - 1, plane_send.at[0]).wait()
+    bytes_of(line1, lines - 1, line_send.at[0]).wait()
     matrix_copy.wait()
     for copy in keep_copies:
         copy.wait()
-    last_sends = middle_sum(1, plane2, line2)
+    middle_sum(1, plane2, line2)
     total = finish_sum(1, line2)
     small_ref[8:16, :] = total[:, 0:D]
     small_ref[24:32, 0:LEN] = total[:, D:WIDTH]
     small_ref[16:32, 3 * LEN : 4 * LEN] = jnp.broadcast_to(live_total, (16, LEN))
     small_ref[16:32, 4 * LEN : D] = jnp.zeros((16, D - 4 * LEN), F32)
-    for copy in last_sends:
-        copy.wait_send()
+    bytes_of(plane2, spots - 1, plane_send.at[1]).wait()
+    bytes_of(line2, lines - 1, line_send.at[1]).wait()
 
 
 def update_kernel(
@@ -888,7 +881,6 @@
     lines = n_wide // 2
     spots = 2 * n_narrow
     blocks = count // GROUP
-    sends = (lines - 1) + lines * n_narrow + lines * (n_narrow - 1)
     anywhere = pl.BlockSpec(memory_space=pl.ANY)
     vmem = pl.BlockSpec(memory_space=pltpu.VMEM)
 
@@ -948,6 +940,7 @@
             pltpu.VMEM((D, D), F32),
             pltpu.VMEM((D, D), BF16),
             pltpu.VMEM((D, D), BF16),
+            pltpu.VMEM((D, D), BF16),
             pltpu.VMEM((count, 16, PACK), BF16),
             pltpu.VMEM((blocks, GROUP * 8, D), BF16),
             pltpu.VMEM((blocks, 16, GROUP * 16), F32),
@@ -956,16 +949,16 @@
             pltpu.VMEM((lines, RANK, WIDTH), F32),
             pltpu.VMEM((spots, RANK, WIDTH), F32),
             pltpu.VMEM((lines, RANK, WIDTH), F32),
-            pltpu.SemaphoreType.DMA((ROWS_DEV,)),
+            pltpu.SemaphoreType.DMA((2,)),
             pltpu.SemaphoreType.DMA,
             pltpu.SemaphoreType.DMA((4,)),
             pltpu.SemaphoreType.DMA,
-            pltpu.SemaphoreType.DMA((sends,)),
+            pltpu.SemaphoreType.DMA,
             pltpu.SemaphoreType.DMA((count,)),
-            pltpu.SemaphoreType.DMA((2, spots)),
-            pltpu.SemaphoreType.DMA((2, spots)),
-            pltpu.SemaphoreType.DMA((2, lines)),
-            pltpu.SemaphoreType.DMA((2, lines)),
+            pltpu.SemaphoreType.DMA((2,)),
+            pltpu.SemaphoreType.DMA((2,)),
+            pltpu.SemaphoreType.DMA((2,)),
+            pltpu.SemaphoreType.DMA((2,)),
         ],
         compiler_params=pltpu.CompilerParams(
             collective_id=0, has_side_effects=True, vmem_limit_bytes=(45 if blocks == 1 else 60) * 2**20

time: 51.5 us -> 50.4 us (0.979)
  Pallas kernels: 49.2 us -> 48.2 us
    pallas_call x1, Pallas kernels: 45.1 us -> 44.1 us  [local(): pl.pallas_call(functools.partial(step_kernel, n_wide, n_narrow), out_shap...]
where the time goes in v5:
time: 50.4 us; the launch traced here: 50.3 us
  Pallas kernels  48.2 us (96%)
  between operations  2.11 us (4%)
    pallas_call x1, Pallas kernels, local(): pl.pallas_call(functools.partial(step_kernel, n_wide, n_narrow), out_shap...  44.1 us
    pallas_call x1, Pallas kernels, local(): pl.pallas_call(functools.partial(update_kernel, count), out_shape=(jax.Sh...  4.09 us

profile of v5, /device:TPU:0, one launch (start us, length us, event | category | flops | bytes accessed | tf_op | source)
XLA Modules:
  0.0 50.3 jit_solution(2561572203846412940)
XLA Ops:
  1.9 44.1 %step.1 = (f32[32,768]{1,0:T(8,128)S(1)}, f32[768,768]{1,0:T(8,128)S(1)}, f32[768,768]{1,0:T(8,128)S(1)}, f32[768,768]{1,0:T(8,128)S(1)}) custom-call(bf16[3,1024,768]{2,1,0:T(8,128)(2,1)} %proj_hbm.1, bf16[1024,768]{1,0:T(8,128)(2,1)} %resid_hbm.1, f32[768,768]{1,0:T(8,128)} %weight_hbm.1, f32[1,768,768]{2,1,0:T(8,128)} %error_hbm.1, ...), custom_call_target="tpu_custom_call" | custom-call | tf_op jit(solution)/shard_map/step/pallas_call | solution.py:891
  46.0 4.1 %update.1 = (f32[768,768]{1,0:T(8,128)}, f32[768,768]{1,0:T(8,128)}, f32[1,768,768]{2,1,0:T(8,128)}, f32[16,128]{1,0:T(8,128)}, f32[16,128]{1,0:T(8,128)}, /*ind...) custom-call(f32[32,768]{1,0:T(8,128)S(1)} %get-tuple-element.22.small_ref, ...), custom_call_target="tpu_custom_call" | custom-call | tf_op jit(solution)/shard_map/update/pallas_call | solution.py:989

commit v6 on v5

--- a/solution.py
+++ b/solution.py
@@ -194,6 +194,7 @@
     out_sem,
     gather_send,
     gather_recv,
+    sibling_recv,
     plane_send,
     plane_recv,
     line_send,
@@ -236,7 +237,7 @@
     def other_line(k):
         return k + (k - line + lines) // lines
 
-    cells = [d for d in offsets if not d[2]]
+    cells = sorted((d for d in offsets if not d[2]), key=lambda d: (-(d[0] > 0) - (d[1] > 0), d[0]))
 
     sibling = (wide, narrow + 1 - 2 * (narrow % 2))
 
@@ -455,27 +456,24 @@
     pl.semaphore_wait(barrier, spots + lines - 2)
     sends = []
 
-    def send_block(block, device):
-        copy = pltpu.make_async_remote_copy(
-            src_ref=gather.at[block],
-            dst_ref=gather.at[block],
-            send_sem=gather_send,
-            recv_sem=gather_recv.at[block],
-            device_id=device,
-            device_id_type=MESH,
-        )
-        copy.start()
-        sends.append(block)
-
-    def await_block(block):
+    def send_block(block, device, arrival=None):
         pltpu.make_async_remote_copy(
             src_ref=gather.at[block],
             dst_ref=gather.at[block],
             send_sem=gather_send,
-            recv_sem=gather_recv.at[block],
-            device_id=sibling,
+            recv_sem=gather_recv.at[block // 2] if arrival is None else arrival,
+            device_id=device,
             device_id_type=MESH,
-        ).wait_recv()
+        ).start()
+        sends.append(block)
+
+    def await_block(block):
+        part = gather.at[block]
+        pltpu.make_async_copy(part, part, gather_recv.at[block // 2]).wait()
+
+    def bytes_of(buffers, blocks, sem):
+        part = buffers.at[pl.ds(0, blocks)]
+        return pltpu.make_async_copy(part, part, sem)
 
     line_order = [line] + [other_line(k) for k in range(lines - 1)]
     for k in far_lines:
@@ -486,7 +484,7 @@
             await_block(block)
         for d in cells:
             send_block(block, spot_device(d)[1])
-        send_block(block, sibling)
+        send_block(block, sibling, sibling_recv)
 
     error_copy.wait()
     factor_parts = stacked_parts(factor_ref[...])
@@ -522,17 +520,9 @@
             _, (other_wide, other_narrow) = spot_device(d)
             block = (line_order[k] * 2 + other_wide % 2) * n_narrow + other_narrow
             await_block(block)
-            send_block(block, sibling)
-    for k in range(lines):
-        for d in [(0, 0, 0)] + cells[::-1]:
-            _, (other_wide, other_narrow) = spot_device(d)
-            block = (
-                (line_order[k] * 2 + other_wide % 2) * n_narrow
-                + other_narrow
-                + 1
-                - 2 * (narrow % 2)
-            )
-            await_block(block)
+            send_block(block, sibling, sibling_recv)
+    bytes_of(gather, count // 2, sibling_recv).wait()
+
     blocks = count // GROUP
     temper = jnp.exp(scale_ref[...])
 
@@ -644,10 +634,6 @@
                 device_id=device,
                 device_id_type=MESH,
             ).start()
-
-    def bytes_of(buffers, blocks, sem):
-        part = buffers.at[pl.ds(0, blocks)]
-        return pltpu.make_async_copy(part, part, sem)
 
     def start_sum(which, plane):
         devices = [spot_device(d)[1] for d in offsets]
@@ -954,7 +940,8 @@
             pltpu.SemaphoreType.DMA((4,)),
             pltpu.SemaphoreType.DMA,
             pltpu.SemaphoreType.DMA,
-            pltpu.SemaphoreType.DMA((count,)),
+            pltpu.SemaphoreType.DMA((count // 2,)),
+            pltpu.SemaphoreType.DMA,
             pltpu.SemaphoreType.DMA((2,)),
             pltpu.SemaphoreType.DMA((2,)),
             pltpu.SemaphoreType.DMA((2,)),

time: 50.4 us -> 50.3 us (level)
  no operation moved by 1% of the time
where the time goes in v6:
time: 50.3 us; the launch traced here: 50.1 us
  Pallas kernels  48 us (95%)
  between operations  2.11 us (4%)
    pallas_call x1, Pallas kernels, local(): pl.pallas_call(functools.partial(step_kernel, n_wide, n_narrow), out_shap...  43.9 us
    pallas_call x1, Pallas kernels, local(): pl.pallas_call(functools.partial(update_kernel, count), out_shape=(jax.Sh...  4.09 us

profile of v6, /device:TPU:0, one launch (start us, length us, event | category | flops | bytes accessed | tf_op | source)
XLA Modules:
  0.0 50.1 jit_solution(9462206501465958957)
XLA Ops:
  1.9 43.9 %step.1 = (f32[32,768]{1,0:T(8,128)S(1)}, f32[768,768]{1,0:T(8,128)S(1)}, f32[768,768]{1,0:T(8,128)S(1)}, f32[768,768]{1,0:T(8,128)S(1)}) custom-call(bf16[3,1024,768]{2,1,0:T(8,128)(2,1)} %proj_hbm.1, bf16[1024,768]{1,0:T(8,128)(2,1)} %resid_hbm.1, f32[768,768]{1,0:T(8,128)} %weight_hbm.1, f32[1,768,768]{2,1,0:T(8,128)} %error_hbm.1, ...), custom_call_target="tpu_custom_call" | custom-call | tf_op jit(solution)/shard_map/step/pallas_call | solution.py:877
  45.9 4.1 %update.1 = (f32[768,768]{1,0:T(8,128)}, f32[768,768]{1,0:T(8,128)}, f32[1,768,768]{2,1,0:T(8,128)}, f32[16,128]{1,0:T(8,128)}, f32[16,128]{1,0:T(8,128)}, /*ind...) custom-call(f32[32,768]{1,0:T(8,128)S(1)} %get-tuple-element.22.small_ref, ...), custom_call_target="tpu_custom_call" | custom-call | tf_op jit(solution)/shard_map/update/pallas_call | solution.py:976

commit v7 on v6

--- a/solution.py
+++ b/solution.py
@@ -395,7 +395,7 @@
         ).astype(BF16)
 
     def project(c):
-        rows = slice(c * 256, (c + 1) * 256)
+        rows = slice(c * 512, (c + 1) * 512)
         zed[rows, :] = resid[rows, :].astype(F32) + tn(mixed_t[:, rows], weight_low[...])
 
     def normalise():
@@ -425,7 +425,7 @@
     weight_copy.wait()
     resid_copy.wait()
     weight_low[...] = weight[...].astype(BF16)
-    for c in range(4):
+    for c in range(2):
         project(c)
     sums = normalise()
     error_copy = load(error_hbm.at[0], error, load_sem.at[1])

time: 50.3 us -> 50.3 us (level)
  no operation moved by 1% of the time
where the time goes in v7:
time: 50.3 us; the launch traced here: 50.1 us
  Pallas kernels  48 us (95%)
  between operations  2.11 us (4%)
    pallas_call x1, Pallas kernels, local(): pl.pallas_call(functools.partial(step_kernel, n_wide, n_narrow), out_shap...  43.9 us
    pallas_call x1, Pallas kernels, local(): pl.pallas_call(functools.partial(update_kernel, count), out_shape=(jax.Sh...  4.09 us

profile of v7, /device:TPU:0, one launch (start us, length us, event | category | flops | bytes accessed | tf_op | source)
XLA Modules:
  0.0 50.1 jit_solution(476979070836891716)
XLA Ops:
  1.9 43.9 %step.1 = (f32[32,768]{1,0:T(8,128)S(1)}, f32[768,768]{1,0:T(8,128)S(1)}, f32[768,768]{1,0:T(8,128)S(1)}, f32[768,768]{1,0:T(8,128)S(1)}) custom-call(bf16[3,1024,768]{2,1,0:T(8,128)(2,1)} %proj_hbm.1, bf16[1024,768]{1,0:T(8,128)(2,1)} %resid_hbm.1, f32[768,768]{1,0:T(8,128)} %weight_hbm.1, f32[1,768,768]{2,1,0:T(8,128)} %error_hbm.1, ...), custom_call_target="tpu_custom_call" | custom-call | tf_op jit(solution)/shard_map/step/pallas_call | solution.py:877
  45.8 4.1 %update.1 = (f32[768,768]{1,0:T(8,128)}, f32[768,768]{1,0:T(8,128)}, f32[1,768,768]{2,1,0:T(8,128)}, f32[16,128]{1,0:T(8,128)}, f32[16,128]{1,0:T(8,128)}, /*ind...) custom-call(f32[32,768]{1,0:T(8,128)S(1)} %get-tuple-element.22.small_ref, ...), custom_call_target="tpu_custom_call" | custom-call | tf_op jit(solution)/shard_map/update/pallas_call | solution.py:976
